TPU v7x, 512 devices: a whole 4x4x16 slice. The times are simulated.
512 devices in a mesh: pipe: 16 (over z), dp: 32 (over x, y, core).
Axes of the slice: x: 4, y: 4, z: 16, core: 2. Of those that a mesh axis runs over, the one named last changes fastest.
Arguments:
- hidden: bfloat16 [4096, 2048], P('dp', 'pipe'), may hold values from -6 to 6
- lengths: int32 [512, 4], P('dp'), may hold values from 1 to 3, as said below
- route: int32 [512, 2], P('dp'), may hold values from 0 to 31, as said below
- gain: float32 [32, 2048], P('pipe'), may hold values from 0.5 to 1.5
- key_weight: bfloat16 [32, 2048, 128], P('pipe'), may hold values from -0.125 to 0.125
- value_weight: bfloat16 [32, 2048, 128], P('pipe'), may hold values from -0.125 to 0.125
- cotangent: bfloat16 [4096, 2048], P('dp'), may hold values from -6 to 6
Outputs:
- input_grad: bfloat16 [4096, 2048], P('dp', 'pipe')
- key_grad: float32 [32, 2048, 128], P('pipe', 'dp')
- value_grad: float32 [32, 2048, 128], P('pipe', 'dp')
Inputs may be any that keep to these rules, and one draw needn't show every extreme that they name: `lengths`: in every micro-batch the first 2 documents fill exactly the first 4 rows, and the others the rest. `route`: for each micro-batch index and each column, the destinations of the 32 groups are all different; and the 32 halves of one group go to 32 different groups.
All inputs are finite; a program needn't handle non-finite values.
Results may differ from a plain program's by a relative error of at most 0.035.
Values may be sent and summed in bfloat16 or wider, within the bound.
A program may use at most 64 MiB of HBM per device.

v0:
```python
import jax
import jax.numpy as jnp
from jax import lax
from jax.sharding import PartitionSpec as P

ROPE_BASE = 500000.0
EPSILON = 1e-05
NEGATIVE = -1e30


def shifted(value, axis, steps):
    count = lax.axis_size(axis)
    pairs = [(source, (source + steps) % count) for source in range(count)]
    return lax.ppermute(value, axis, pairs)


def spread(value, axis, root):
    mine = lax.axis_index(axis) == root
    return lax.psum(jnp.where(mine, value, jnp.zeros_like(value)), axis)


def document_positions(lengths, row_count):
    doc_ends = jnp.cumsum(lengths, axis=-1)
    doc_starts = doc_ends - lengths
    row_numbers = jnp.arange(row_count, dtype=jnp.int32)
    document = jnp.sum(
        (row_numbers[None, :, None] >= doc_ends[:, None, :-1]).astype(jnp.int32),
        axis=-1,
        dtype=jnp.int32,
    )
    picked = document[:, :, None] == jnp.arange(lengths.shape[1], dtype=jnp.int32)[None, None, :]
    opening = jnp.sum(jnp.where(picked, doc_starts[:, None, :], 0), axis=-1, dtype=jnp.int32)
    return (document, row_numbers[None, :] - opening)


def rotary_tables(position, head_size):
    frequency = ROPE_BASE ** (-(jnp.arange(head_size // 2, dtype=jnp.float32) * 2.0 / head_size))
    angles = position.astype(jnp.float32)[..., None] * frequency
    return (jnp.cos(angles), jnp.sin(angles))


def rotate(vectors, cosine_table, sine_table):
    midpoint = vectors.shape[-1] // 2
    front_half = vectors[..., :midpoint]
    rear_half = vectors[..., midpoint:]
    return jnp.concatenate(
        [
            front_half * cosine_table - rear_half * sine_table,
            rear_half * cosine_table + front_half * sine_table,
        ],
        axis=-1,
    )


def normalize(hidden_in, gain_row):
    return (
        hidden_in
        * lax.rsqrt(jnp.mean(hidden_in * hidden_in, axis=-1, keepdims=True) + EPSILON)
        * gain_row
    )


def attend_layer(
    hidden_in,
    gain_row,
    key_proj,
    value_proj,
    key_zero,
    value_zero,
    document,
    position,
    cosine_table,
    sine_table,
):
    batch_count, row_count, feature_count = hidden_in.shape
    head_size = key_proj.shape[1]
    head_count = feature_count // head_size
    normed = normalize(hidden_in, gain_row)
    packed = normed.astype(jnp.bfloat16)
    flattened = packed.reshape(batch_count * row_count, feature_count)
    key_pre = (
        jnp.dot(flattened, key_proj, preferred_element_type=jnp.float32).reshape(
            batch_count, row_count, head_size
        )
        + key_zero
    )
    value_pre = (
        jnp.dot(flattened, value_proj, preferred_element_type=jnp.float32).reshape(
            batch_count, row_count, head_size
        )
        + value_zero
    )
    queries = rotate(
        normed.reshape(batch_count, row_count, head_count, head_size),
        cosine_table[:, :, None, :],
        sine_table[:, :, None, :],
    ).astype(jnp.bfloat16)
    key_vecs = rotate(key_pre, cosine_table, sine_table).astype(jnp.bfloat16)
    values = value_pre.astype(jnp.bfloat16)
    scores = jnp.einsum(
        "bshd,btd->bhst", queries, key_vecs, preferred_element_type=jnp.float32
    ) * head_size ** (-0.5)
    allowed = (document[:, :, None] == document[:, None, :]) & (
        position[:, None, :] <= position[:, :, None]
    )
    scores = jnp.where(allowed[:, None, :, :], scores, NEGATIVE)
    ceiling = lax.stop_gradient(jnp.max(scores, axis=-1, keepdims=True))
    raised = jnp.exp(scores - ceiling)
    weights = (raised / jnp.sum(raised, axis=-1, keepdims=True)).astype(jnp.bfloat16)
    mixture = jnp.einsum(
        "bhst,btd->bshd", weights, values, preferred_element_type=jnp.float32
    ).reshape(batch_count, row_count, feature_count)
    return hidden_in + mixture


def select_row(array, index_value):
    return lax.dynamic_index_in_dim(array, index_value, 0, keepdims=False)


def section_hop(payload, offset):
    return shifted(payload, "pipe", offset)


def body(hidden, lengths, route, gain, key_weight, value_weight, cotangent):
    group_count = lax.axis_size("dp")
    section_count = lax.axis_size("pipe")
    section_index = lax.axis_index("pipe")
    micro_count, doc_count = lengths.shape
    source_rows, column_count = hidden.shape
    row_count = source_rows // micro_count
    half_rows = row_count // 2
    half_count = 2 * micro_count
    feature_count = gain.shape[1]
    head_size = key_weight.shape[2]
    document, position = document_positions(lengths, row_count)
    row_tags = (document * row_count + position).reshape(half_count, half_rows)
    own_halves = hidden.reshape(half_count, half_rows, column_count)
    route_flat = route.reshape(half_count)
    send_order = jnp.argsort(route_flat)
    outgoing = own_halves[send_order]
    outgoing_tags = row_tags[send_order]
    arrived, arrived_tags, arrived_slots = (
        lax.all_to_all(outgoing, "dp", split_axis=0, concat_axis=0, tiled=True),
        lax.all_to_all(outgoing_tags, "dp", split_axis=0, concat_axis=0, tiled=True),
        lax.all_to_all(send_order, "dp", split_axis=0, concat_axis=0, tiled=True),
    )
    placing = jnp.argsort(arrived_slots)
    received = arrived[placing].reshape(micro_count, row_count, column_count)
    recv_tags = arrived_tags[placing].reshape(micro_count, row_count)
    recv_document = recv_tags // row_count
    recv_position = recv_tags % row_count
    cosine_table, sine_table = rotary_tables(recv_position, head_size)
    full_rows = lax.all_gather(
        received.reshape(micro_count * row_count, column_count), "pipe", axis=1, tiled=True
    )
    full_rows = full_rows.reshape(micro_count, row_count, feature_count).astype(jnp.float32)
    upstream_all = cotangent.reshape(micro_count, row_count, feature_count).astype(jnp.float32)
    tick_count = 2 * section_count + micro_count - 1
    zero_index = jnp.zeros((), jnp.int32)
    zero_terms = jnp.zeros((1, row_count, head_size), jnp.float32)

    def layer_inputs(virtual, micro_index):
        return (
            select_row(gain, virtual),
            select_row(key_weight, virtual),
            select_row(value_weight, virtual),
            lax.dynamic_index_in_dim(recv_document, micro_index, 0, True),
            lax.dynamic_index_in_dim(recv_position, micro_index, 0, True),
            lax.dynamic_index_in_dim(cosine_table, micro_index, 0, True),
            lax.dynamic_index_in_dim(sine_table, micro_index, 0, True),
        )

    def forward_tick(tick, carry):
        incoming, saved = carry
        first_pass = tick - section_index
        second_pass = first_pass - section_count
        use_first = (first_pass >= 0) & (first_pass < micro_count)
        use_second = (second_pass >= 0) & (second_pass < micro_count)
        active = use_first | use_second
        virtual = use_second.astype(jnp.int32)
        micro_index = jnp.clip(jnp.where(use_second, second_pass, first_pass), 0, micro_count - 1)
        current = jnp.where(
            (section_index == 0) & use_first, select_row(full_rows, micro_index), incoming
        )
        gain_row, key_proj, value_proj, doc_rows, pos_rows, cos_rows, sin_rows = layer_inputs(
            virtual, micro_index
        )
        produced = attend_layer(
            current[None],
            gain_row,
            key_proj,
            value_proj,
            zero_terms,
            zero_terms,
            doc_rows,
            pos_rows,
            cos_rows,
            sin_rows,
        )[0]
        previous = saved[virtual, micro_index]
        saved = lax.dynamic_update_slice(
            saved,
            jnp.where(active, current, previous)[None, None],
            (virtual, micro_index, zero_index, zero_index),
        )
        return (section_hop(produced, 1), saved)

    forward_start = (
        jnp.zeros((row_count, feature_count), jnp.float32),
        jnp.zeros((2, micro_count, row_count, feature_count), jnp.float32),
    )
    leftover, saved = lax.fori_loop(0, tick_count, forward_tick, forward_start)

    def backward_tick(tick, carry):
        incoming, terms, input_grads = carry
        second_pass = tick - (section_count - 1 - section_index)
        first_pass = second_pass - section_count
        use_first = (first_pass >= 0) & (first_pass < micro_count)
        use_second = (second_pass >= 0) & (second_pass < micro_count)
        active = use_first | use_second
        virtual = use_second.astype(jnp.int32)
        micro_index = jnp.clip(jnp.where(use_second, second_pass, first_pass), 0, micro_count - 1)
        upstream = jnp.where(
            (section_index == section_count - 1) & use_second,
            select_row(upstream_all, micro_index),
            incoming,
        )
        stored = saved[virtual, micro_index]
        gain_row, key_proj, value_proj, doc_rows, pos_rows, cos_rows, sin_rows = layer_inputs(
            virtual, micro_index
        )

        def pull_layer():

            def local_layer(layer_in, key_zero, value_zero):
                return attend_layer(
                    layer_in,
                    gain_row,
                    key_proj,
                    value_proj,
                    key_zero,
                    value_zero,
                    doc_rows,
                    pos_rows,
                    cos_rows,
                    sin_rows,
                )

            layer_out, pullback = jax.vjp(local_layer, stored[None], zero_terms, zero_terms)
            grad_rows, key_part, value_part = pullback(upstream[None])
            return (
                grad_rows[0],
                jnp.concatenate([key_part[0], value_part[0]], axis=-1).astype(jnp.bfloat16),
            )

        grad_rows, pair_terms = pull_layer()
        previous_terms = terms[virtual, micro_index]
        terms = lax.dynamic_update_slice(
            terms,
            jnp.where(active, pair_terms, previous_terms)[None, None],
            (virtual, micro_index, zero_index, zero_index),
        )
        keep_grad = (section_index == 0) & use_first
        previous_grad = input_grads[micro_index]
        input_grads = lax.dynamic_update_slice(
            input_grads,
            jnp.where(keep_grad, grad_rows, previous_grad)[None],
            (micro_index, zero_index, zero_index),
        )
        return (section_hop(grad_rows, -1), terms, input_grads)

    backward_start = (
        jnp.zeros((row_count, feature_count), jnp.float32),
        jnp.zeros((2, micro_count, row_count, 2 * head_size), jnp.bfloat16),
        jnp.zeros((micro_count, row_count, feature_count), jnp.float32),
    )
    leftover, terms, input_grads = lax.fori_loop(0, tick_count, backward_tick, backward_start)
    packed_all = normalize(saved, gain[:, None, None, :]).astype(jnp.bfloat16)
    summed = lax.psum_scatter(
        jnp.einsum("vmsw,vmsc->wvc", packed_all, terms, preferred_element_type=jnp.float32).reshape(
            feature_count, 4 * head_size
        ),
        "dp",
        scatter_dimension=0,
        tiled=True,
    )
    summed = summed.reshape(feature_count // group_count, 2, 2, head_size)
    key_out = jnp.transpose(summed[:, :, 0, :], (1, 0, 2))
    value_out = jnp.transpose(summed[:, :, 1, :], (1, 0, 2))
    everywhere = spread(input_grads.astype(jnp.bfloat16), "pipe", 0)
    own_grads = lax.dynamic_slice_in_dim(everywhere, section_index * column_count, column_count, 2)
    grad_halves = own_grads.reshape(half_count, half_rows, column_count)
    returning = grad_halves[arrived_slots]
    returned = lax.all_to_all(returning, "dp", split_axis=0, concat_axis=0, tiled=True)
    source_grad = returned[route_flat]
    return (source_grad.reshape(source_rows, column_count), key_out, value_out)


def solution(mesh):
    placed = (
        P("dp", "pipe"),
        P("dp", None),
        P("dp", None),
        P("pipe", None),
        P("pipe", None, None),
        P("pipe", None, None),
        P("dp", None),
    )
    return jax.shard_map(
        body,
        mesh=mesh,
        in_specs=placed,
        out_specs=(P("dp", "pipe"), P("pipe", "dp", None), P("pipe", "dp", None)),
        check_vma=False,
    )
```

profile of v0, /device:TPU:1, one launch (start us, length us, event | category | flops | bytes accessed | tf_op | source)
XLA Modules:
  0.0 1585.1 jit_solution(1690798589335721596)
XLA Ops:
  11.2 10.4 all-to-all-start.1
  28.5 6.8 all-to-all-start
  48.3 5.4 all-to-all-done.2
  54.4 29.6 %all_gather.3 = bf16[128,2048]{1,0:T(8,128)(2,1)S(1)} all-gather(bf16[128,128]{1,0:T(8,128)(2,1)S(1)} %bitcast.400), channel_id=1, replica_groups=mesh['pipe'=16,'dp'=32] {'pipe'}, dimensions={1}, use_global_device_ids=true | all-gather | bytes 557056 | tf_op jit(solution)/shard_map/all_gather | solution.py:153
  85.8 467.4 %while.36 = (s32[]{:T(128)}, f32[8,2048]{1,0:T(8,128)S(1)}, f32[2,16,8,2048]{3,2,1,0:T(8,128)}, s32[]{:T(128)}, pred[]{:T(512)}, /*index=5*/f32[16,8,2048]{2,1,0...) while((s32[]{:T(128)}, f32[8,2048]{1,0:T(8,128)S(1)}, ...), condition=%wide.region_9.10_spmd, body=%wide.region_5.9_spmd.sunk | while | flops 9274331 | bytes 2739535 | solution.py:212
  121.0 5.2 collective-permute-done
  220.7 5.0 collective-permute-done
  555.1 758.4 %while.37 = (s32[]{:T(128)}, f32[8,2048]{1,0:T(8,128)S(1)}, bf16[2,16,8,256]{3,2,1,0:T(8,128)(2,1)S(1)}, bf16[16,8,2048]{2,1,0:T(8,128)(2,1)S(1)}, s32[]{:T(128)...) while((s32[]{:T(128)}, f32[8,2048]{1,0:T(8,128)S(1)}, ...), condition=%wide.region_16.17_spmd, body=%wide.region_10.16_spmd.sunk | while | flops 18770692 | bytes 4485175 | solution.py:277
  610.6 4.9 collective-permute-start.1
  626.7 4.9 collective-permute-start.1
  642.9 4.9 collective-permute-start.1
  659.0 4.9 collective-permute-start.1
  675.2 4.9 collective-permute-start.1
  691.4 4.9 collective-permute-start.1
  707.8 5.3 collective-permute-start.1
  724.3 4.9 collective-permute-start.1
  740.5 4.9 collective-permute-start.1
  756.7 4.9 collective-permute-start.1
  789.0 4.9 collective-permute-start.1
  805.1 4.9 collective-permute-start.1
  821.3 4.9 collective-permute-start.1
  837.4 4.9 collective-permute-start.1
  853.6 4.9 collective-permute-start.1
  869.8 4.9 collective-permute-start.1
  902.1 4.9 collective-permute-start.1
  918.2 4.9 collective-permute-start.1
  934.4 4.9 collective-permute-start.1
  951.1 5.3 collective-permute-start.1
  967.6 4.9 collective-permute-start.1
  983.8 4.9 collective-permute-start.1
  1000.0 4.9 collective-permute-start.1
  1016.1 4.9 collective-permute-start.1
  1048.4 4.9 collective-permute-start.1
  1064.6 4.9 collective-permute-start.1
  1080.7 4.9 collective-permute-start.1
  1096.9 4.9 collective-permute-start.1
  1113.1 4.9 collective-permute-start.1
  1129.2 4.9 collective-permute-start.1
  1145.4 4.9 collective-permute-start.1
  1161.5 4.9 collective-permute-start.1
  1177.7 4.9 collective-permute-start.1
  1194.1 5.1 collective-permute-start.1
  1210.4 4.9 collective-permute-start.1
  1226.5 4.9 collective-permute-start.1
  1318.8 5.3 copy.92
  1324.9 222.9 %all-reduce.6.cloned.1.call-done = bf16[16,8,2048]{2,1,0:T(8,128)(2,1)} async-done(((bf16[16,8,2048]{2,1,0:T(8,128)(2,1)}), bf16[16,8,2048]{2,1,0:T(8,128)(2,1)}) %all-reduce.6.cloned.1.call-update) | async-done | bytes 524304 | tf_op jit(solution)/shard_map/psum | solution.py:19
  1549.8 17.0 %all-to-all-start.3 = ((bf16[32,4,128]{2,1,0:T(4,128)(2,1)}), bf16[32,4,128]{2,1,0:T(4,128)(2,1)S(1)}, u32[]{:S(2)}, u32[]{:S(2)}) async-start(bf16[32,4,128]{2,1,0:T(4,128)(2,1)} %gather_fusion.4), calls=%async_computation.3 | async-start | bytes 65536 | tf_op jit(solution)/shard_map/all_to_all | solution.py:294
  1566.8 7.3 all-to-all-done.3
  (2391 shorter events, 1067.9 us)
Async XLA Ops:
  11.2 17.3 %all-to-all-start.1 = ((s32[32,1,1]{2,1,0:T(1,128)}), s32[32,1,1]{2,1,0:T(1,128)S(1)}, u32[]{:S(2)}, u32[]{:S(2)}) async-start(s32[32,1,1]{2,1,0:T(1,128)} %copy.80), calls=%async_computation.1 | async-start | bytes 32768 | tf_op jit(solution)/shard_map/all_to_all | solution.py:145
  28.5 13.7 all-to-all-start
  42.2 11.6 all-to-all-start.2
  46.4 1501.4 %all-reduce.6.cloned.1.call-start = ((), (), s32[]{:S(2)}) async-start(), calls=%async_computation.5 | async-start | bytes 1048576 | tf_op jit(solution)/shard_map/psum | solution.py:19
  119.1 7.1 collective-permute-start
  218.7 6.9 collective-permute-start
  308.3 6.3 collective-permute-start
  318.2 6.8 collective-permute-start
  407.6 6.4 collective-permute-start
  417.7 6.6 collective-permute-start
  507.1 6.5 collective-permute-start
  610.6 6.2 collective-permute-start.1
  626.7 6.2 collective-permute-start.1
  642.9 6.2 collective-permute-start.1
  659.0 6.2 collective-permute-start.1
  675.2 6.2 collective-permute-start.1
  691.4 6.5 collective-permute-start.1
  707.8 6.6 collective-permute-start.1
  724.3 6.2 collective-permute-start.1
  740.5 6.2 collective-permute-start.1
  756.7 6.2 collective-permute-start.1
  772.8 6.2 collective-permute-start.1
  789.0 6.2 collective-permute-start.1
  805.1 6.2 collective-permute-start.1
  821.3 6.2 collective-permute-start.1
  837.4 6.2 collective-permute-start.1
  869.8 6.2 collective-permute-start.1
  902.1 6.2 collective-permute-start.1
  918.2 6.2 collective-permute-start.1
  934.4 6.8 collective-permute-start.1
  951.1 6.6 collective-permute-start.1
  983.8 6.2 collective-permute-start.1
  1016.1 6.2 collective-permute-start.1
  1048.4 6.2 collective-permute-start.1
  1064.6 6.2 collective-permute-start.1
  1096.9 6.2 collective-permute-start.1
  1129.2 6.2 collective-permute-start.1
  1145.4 6.2 collective-permute-start.1
  1161.5 6.2 collective-permute-start.1
  1177.7 6.4 collective-permute-start.1
  1194.1 6.4 collective-permute-start.1
  1210.4 6.2 collective-permute-start.1
  1242.7 6.2 collective-permute-start.1
  1258.8 6.2 collective-permute-start.1
  1275.0 6.2 collective-permute-start.1
  1291.2 6.2 collective-permute-start.1
  1314.4 260.9 %reduce-scatter.2.cloned.1.call-start = ((), (), s32[]{:S(2)}) async-start(), calls=%async_computation.6 | async-start | bytes 4325376 | tf_op jit(solution)/shard_map/reduce_scatter | solution.py:279
  1549.8 24.3 %all-to-all-start.3 = ((bf16[32,4,128]{2,1,0:T(4,128)(2,1)}), bf16[32,4,128]{2,1,0:T(4,128)(2,1)S(1)}, u32[]{:S(2)}, u32[]{:S(2)}) async-start(bf16[32,4,128]{2,1,0:T(4,128)(2,1)} %gather_fusion.4), calls=%async_computation.3 | async-start | bytes 65536 | tf_op jit(solution)/shard_map/all_to_all | solution.py:294
  (58 other events, 452.3 us)
Sparse Core Ops, SparseCore 0:
  1314.6 233.2 all-reduce.5
Sparse Core Ops, SparseCore 1:
  1324.3 209.4 reduce-scatter.1
where the time goes:
time: 1610 us; the launch traced here: 1590 us
  waiting for transfers between devices  506 us (31%)
  starting transfers between devices  355 us (22%)
  other arithmetic  334 us (21%)
  matrix products  267 us (17%)
  local copies, waits for them, and re-layouts  68.3 us (4%)
  blocking collectives  29.6 us (2%)
    ppermute x94, starting transfers between devices, shifted(): return lax.ppermute(value, axis, pairs)  316 us
    ppermute x94, waiting for transfers between devices, shifted(): return lax.ppermute(value, axis, pairs)  265 us
    psum x1, waiting for transfers between devices, spread(): return lax.psum(jnp.where(mine, value, jnp.zeros_like(value)), axis)  223 us
    dot_general x141, matrix products, attend_layer(): jnp.einsum('bhst,btd->bshd', weights, values, preferred_element_type=jnp....  87.5 us
    concatenate x235, other arithmetic, rotate(): jnp.concatenate([front_half * cosine_table - rear_half * sine_table, rear...  84.4 us
    dot_general x141, matrix products, attend_layer(): jnp.dot(flattened, key_proj, preferred_element_type=jnp.float32)  74.1 us
    dot_general x47, matrix products, attend_layer(): jnp.dot(flattened, value_proj, preferred_element_type=jnp.float32)  56.6 us
    while x141, other arithmetic  54.5 us
  transfers between devices with their start and end apart: 100, of which 99 were waited for; matrix products, arithmetic and copies ran while one was open for 2% of the time, Pallas kernels for 0%

commit v1 on v0

v1 whole, which is shorter than its diff:
```python
import jax
import jax.numpy as jnp
from jax import lax
from jax.experimental import pallas as pl
from jax.experimental.pallas import tpu as pltpu
from jax.sharding import PartitionSpec as P

ROPE_BASE = 500000.0
EPSILON = 1e-05
NEGATIVE = -1e30
HEADS = 16
ROWS = 8
HEAD = 128
F32 = jnp.float32
BF16 = jnp.bfloat16


def document_positions(lengths, row_count):
    doc_ends = jnp.cumsum(lengths, axis=-1)
    doc_starts = doc_ends - lengths
    row_numbers = jnp.arange(row_count, dtype=jnp.int32)
    document = jnp.sum(
        (row_numbers[None, :, None] >= doc_ends[:, None, :-1]).astype(jnp.int32),
        axis=-1,
        dtype=jnp.int32,
    )
    picked = document[:, :, None] == jnp.arange(lengths.shape[1], dtype=jnp.int32)[None, None, :]
    opening = jnp.sum(jnp.where(picked, doc_starts[:, None, :], 0), axis=-1, dtype=jnp.int32)
    return (document, row_numbers[None, :] - opening)


def dot(a, b, over_a, over_b):
    return lax.dot_general(
        a, b, (((over_a,), (over_b,)), ((), ())), preferred_element_type=F32
    )


def swap_halves(flat):
    return pltpu.roll(flat, HEAD // 2, 1)


def turn(flat, cosine, sine):
    return flat * cosine + swap_halves(flat) * sine


def unturn(flat, cosine, sine):
    return flat * cosine - swap_halves(flat) * sine


def side_by_side(flat):
    return jnp.concatenate([flat[ROWS * h:ROWS * (h + 1)] for h in range(HEADS)], axis=1)


def stacked(wide):
    return jnp.concatenate([wide[:, HEAD * h:HEAD * (h + 1)] for h in range(HEADS)], axis=0)


def row_mean(flat):
    total = jnp.sum(flat.reshape(HEADS, ROWS, HEAD), axis=0)
    return jnp.sum(total, axis=-1, keepdims=True) * (1.0 / (HEADS * HEAD))


def over_heads(rows):
    return jnp.broadcast_to(rows[None], (HEADS, ROWS, rows.shape[-1])).reshape(
        HEADS * ROWS, rows.shape[-1]
    )


def gain_rows(gain):
    return jnp.broadcast_to(gain[:, None, :], (HEADS, ROWS, HEAD)).reshape(HEADS * ROWS, HEAD)


def layers_kernel(
    start_ref, last_ref, cos_ref, sin_ref, bias_ref, gain_ref, weight_ref,
    packed_ref, pair_ref, grad_ref,
    current, saved, saved_queries, saved_keys, saved_weights, saved_scale,
):
    step = pl.program_id(0)
    layers = gain_ref.shape[0]
    weight = weight_ref[...].reshape(HEADS * HEAD, 2 * HEAD)
    cosine, sine = cos_ref[...], sin_ref[...]
    cosine_all, sine_all = over_heads(cosine), over_heads(sine)

    @pl.when(step == 0)
    def _():
        current[...] = start_ref[...].astype(F32)

    @pl.when(step < layers)
    def _():
        x = current[...]
        saved[step] = x
        scale = lax.rsqrt(row_mean(x * x) + EPSILON)
        saved_scale[step] = scale
        normed = x * over_heads(scale) * gain_rows(gain_ref[step])
        packed = side_by_side(normed).astype(BF16)
        packed_ref[step] = packed
        pre = dot(packed, weight, 1, 0)
        keys = turn(pre[:, :HEAD], cosine, sine).astype(BF16)
        values = pre[:, HEAD:].astype(BF16)
        queries = turn(normed, cosine_all, sine_all).astype(BF16)
        scores = dot(keys, queries, 1, 1) * HEAD ** (-0.5) + bias_ref[...]
        raised = jnp.exp(scores - jnp.max(scores, axis=0, keepdims=True))
        weights = raised / jnp.sum(raised, axis=0, keepdims=True)
        saved_queries[step] = queries
        saved_keys[step, 0] = keys
        saved_keys[step, 1] = values
        saved_weights[step] = weights
        current[...] = x + dot(weights.astype(BF16), values, 0, 0)

    @pl.when(step == layers)
    def _():
        current[...] = last_ref[...].astype(F32)

    @pl.when(step >= layers)
    def _():
        layer = 2 * layers - 1 - step
        upstream = current[...]
        rounded = upstream.astype(BF16)
        keys = saved_keys[layer, 0]
        values = saved_keys[layer, 1]
        weights = saved_weights[layer]
        d_weights = dot(values, rounded, 1, 1).astype(BF16).astype(F32)
        d_values = dot(weights.astype(BF16), rounded, 1, 0).astype(BF16).astype(F32)
        inner = jnp.sum(d_weights * weights, axis=0, keepdims=True)
        d_scores = (weights * (d_weights - inner) * HEAD ** (-0.5)).astype(BF16)
        d_queries = dot(d_scores, keys, 0, 0).astype(BF16).astype(F32)
        d_keys = dot(d_scores, saved_queries[layer], 1, 0).astype(BF16).astype(F32)
        d_key_pre = unturn(d_keys, cosine, sine)
        pair = jnp.concatenate([d_key_pre, d_values], axis=1).astype(BF16)
        pair_ref[layer] = pair
        d_packed = stacked(dot(pair, weight, 1, 1))
        d_normed = unturn(d_queries, cosine_all, sine_all) + d_packed
        x = saved[layer]
        scale = saved_scale[layer]
        scaled = d_normed * gain_rows(gain_ref[layer])
        pull = row_mean(scaled * x) * scale * scale * scale
        current[...] = upstream + scaled * over_heads(scale) - x * over_heads(pull)

    @pl.when(step == 2 * layers - 1)
    def _():
        grad_ref[...] = current[...].astype(BF16)


def run_layers(start, last, cosine, sine, bias, gain, weight, sections, features, interpret=False):
    layers = gain.shape[0]
    parts = weight.shape[0]

    def block_of(step):
        layer = jnp.where(step < layers, step, 2 * layers - 1 - step)
        return (0, layer % sections, layer // sections, 0, 0)

    whole = pl.BlockSpec(memory_space=pltpu.VMEM)
    tile = HEADS * ROWS
    return pl.pallas_call(
        layers_kernel,
        grid=(2 * layers,),
        out_shape=(
            jax.ShapeDtypeStruct((layers, ROWS, HEADS * HEAD), BF16),
            jax.ShapeDtypeStruct((layers, ROWS, 2 * HEAD), BF16),
            jax.ShapeDtypeStruct((tile, HEAD), BF16),
        ),
        in_specs=[whole] * 6
        + [pl.BlockSpec((parts, 1, 1, features // parts, 2 * HEAD), block_of)],
        out_specs=(whole, whole, whole),
        scratch_shapes=[
            pltpu.VMEM((tile, HEAD), F32),
            pltpu.VMEM((layers, tile, HEAD), F32),
            pltpu.VMEM((layers, tile, HEAD), BF16),
            pltpu.VMEM((layers, 2, ROWS, HEAD), BF16),
            pltpu.VMEM((layers, ROWS, tile), F32),
            pltpu.VMEM((layers, ROWS, 1), F32),
        ],
        compiler_params=pltpu.CompilerParams(vmem_limit_bytes=40 * 2**20),
        interpret=interpret,
    )(start, last, cosine, sine, bias, gain, weight)


def attention_tables(document, position):
    half = HEAD // 2
    frequency = ROPE_BASE ** (-(jnp.arange(half, dtype=F32) * 2.0 / HEAD))
    angles = position.astype(F32)[:, None] * frequency
    cosine, sine = jnp.cos(angles), jnp.sin(angles)
    allowed = (document[:, None] == document[None, :]) & (position[:, None] <= position[None, :])
    bias = jnp.where(allowed, 0.0, NEGATIVE).astype(F32)
    return (
        jnp.concatenate([cosine, cosine], axis=-1),
        jnp.concatenate([-sine, sine], axis=-1),
        jnp.tile(bias, (1, HEADS)),
    )


def body(hidden, lengths, route, gain, key_weight, value_weight, cotangent):
    groups = lax.axis_size("dp")
    sections = lax.axis_size("pipe")
    group = lax.axis_index("dp")
    section = lax.axis_index("pipe")
    micro_count = lengths.shape[0]
    source_rows, columns = hidden.shape
    half_rows = ROWS // 2
    half_count = 2 * micro_count
    features = gain.shape[1]
    part = features // groups

    both = jnp.concatenate([key_weight, value_weight], axis=-1)
    share = lax.dynamic_slice_in_dim(both, group * part, part, 1)
    column = lax.all_gather(share, "pipe", axis=0, tiled=False)
    weight = lax.all_gather(column, "dp", axis=0, tiled=False)
    gains = lax.all_gather(gain, "pipe", axis=0, tiled=False)
    gains = jnp.swapaxes(gains, 0, 1).reshape(2 * sections, HEADS, HEAD)

    document, position = document_positions(lengths, ROWS)
    tags = (document * ROWS + position).reshape(half_count, half_rows)
    slots = jnp.arange(half_count, dtype=jnp.int32)
    route_flat = route.reshape(half_count)
    label = jnp.concatenate([tags, slots[:, None]], axis=1)
    label = jnp.pad(label, ((0, 0), (0, columns - half_rows - 1))).astype(BF16)
    packet = jnp.concatenate([hidden.reshape(half_count, half_rows * columns), label], axis=1)
    chosen = (route_flat[None, :] == jnp.arange(groups, dtype=jnp.int32)[:, None]).astype(BF16)
    outgoing = jnp.dot(chosen, packet, preferred_element_type=F32).astype(BF16)
    arrived = lax.all_to_all(outgoing, "dp", split_axis=0, concat_axis=0, tiled=True)
    arrived_label = arrived[:, half_rows * columns:]
    arrived_slots = arrived_label[:, half_rows].astype(jnp.int32)
    placing = (arrived_slots[None, :] == slots[:, None]).astype(BF16)
    received = jnp.dot(placing, arrived, preferred_element_type=F32).astype(BF16)
    row_tags = received[:, half_rows * columns:half_rows * columns + half_rows]
    row_tags = row_tags.astype(jnp.int32).reshape(micro_count, ROWS)
    own_tags = lax.dynamic_index_in_dim(row_tags, section, 0, keepdims=False)
    rows = received[:, :half_rows * columns].reshape(micro_count, ROWS, columns)
    start = lax.all_to_all(rows, "pipe", split_axis=0, concat_axis=0, tiled=True)
    start = start.reshape(HEADS * ROWS, HEAD)
    cosine, sine, bias = attention_tables(own_tags // ROWS, own_tags % ROWS)
    last = lax.dynamic_slice_in_dim(cotangent, section * ROWS, ROWS, 0)
    last = jnp.swapaxes(last.reshape(ROWS, HEADS, HEAD), 0, 1).reshape(HEADS * ROWS, HEAD)

    packed, pairs, grads = run_layers(
        start, last, cosine, sine, bias, gains, weight, sections, features
    )

    mine = lax.all_to_all(
        grads.reshape(sections, ROWS, columns), "pipe", split_axis=0, concat_axis=0, tiled=True
    )
    mine = mine.reshape(half_count, half_rows * columns)
    returning = jnp.dot(placing.T, mine, preferred_element_type=F32).astype(BF16)
    returned = lax.all_to_all(returning, "dp", split_axis=0, concat_axis=0, tiled=True)
    source_grad = jnp.dot(chosen.T, returned, preferred_element_type=F32).astype(BF16)

    layer_packed = lax.all_to_all(
        packed.reshape(2, sections, ROWS, features), "pipe", split_axis=1, concat_axis=1, tiled=True
    )
    layer_pairs = lax.all_to_all(
        pairs.reshape(2, sections, ROWS, 2 * HEAD), "pipe", split_axis=1, concat_axis=1, tiled=True
    )
    terms = jnp.einsum("vmsw,vmsc->wvc", layer_packed, layer_pairs, preferred_element_type=F32)
    summed = lax.psum_scatter(
        terms.astype(BF16).reshape(features, 4 * HEAD), "dp", scatter_dimension=0, tiled=True
    )
    summed = summed.astype(F32).reshape(part, 2, 2, HEAD)
    key_out = jnp.transpose(summed[:, :, 0, :], (1, 0, 2))
    value_out = jnp.transpose(summed[:, :, 1, :], (1, 0, 2))
    return (source_grad.reshape(source_rows, columns), key_out, value_out)


def solution(mesh):
    placed = (
        P("dp", "pipe"),
        P("dp", None),
        P("dp", None),
        P("pipe", None),
        P("pipe", None, None),
        P("pipe", None, None),
        P("dp", None),
    )
    return jax.shard_map(
        body,
        mesh=mesh,
        in_specs=placed,
        out_specs=(P("dp", "pipe"), P("pipe", "dp", None), P("pipe", "dp", None)),
        check_vma=False,
    )
```

time: 1610 us -> 479 us (0.30); the launches traced: 1590 us -> 477 us
  other arithmetic: 334 us -> 3.43 us
  starting transfers between devices: 355 us -> 34.7 us
  waiting for transfers between devices: 506 us -> 228 us
  matrix products: 267 us -> 1.38 us
  blocking collectives: 29.6 us -> 115 us
  Pallas kernels: 0 us -> 70.9 us
  local copies, waits for them, and re-layouts: 68.3 us -> 9.43 us
    ppermute x94 -> x0, starting transfers between devices: 316 us -> none  [shifted(): return lax.ppermute(value, axis, pairs)]
    dot_general x518 -> x5, matrix products: 267 us -> 1.38 us  [the longest x1 0.75 us: body(): jnp.einsum('vmsw,vmsc->wvc', layer_packed, layer_pairs, preferred_element...]
    ppermute x94 -> x0, waiting for transfers between devices: 265 us -> none  [shifted(): return lax.ppermute(value, axis, pairs)]
    psum x1 -> x0, waiting for transfers between devices: 223 us -> none  [spread(): return lax.psum(jnp.where(mine, value, jnp.zeros_like(value)), axis)]
    all_gather x0 -> x2, waiting for transfers between devices: none -> 144 us  [the longest x1 75.4 us: body(): weight = lax.all_gather(column, 'dp', axis=0, tiled=False)]
    all_to_all x0 -> x3, blocking collectives: none -> 89.4 us  [the longest x1 51.5 us: body(): lax.all_to_all(packed.reshape(2, sections, ROWS, features), 'pipe', split...]
    concatenate x282 -> x3, other arithmetic: 87.9 us -> 1.6 us  [the longest x1 1.51 us: body(): both = jnp.concatenate([key_weight, value_weight], axis=-1)]
    dynamic_update_slice x141 -> x0, other arithmetic: 74.6 us -> none  [the longest x47 43.9 us: backward_tick(): lax.dynamic_update_slice(input_grads, jnp.where(keep_grad, grad_rows, pre...]
  transfers between devices with their start and end apart: 100 -> 6, of which waited for: 99 -> 5; matrix products, arithmetic and copies ran while one was open for 2% -> 1% of each run, Pallas kernels for 0% -> 0%
where the time goes in v1:
time: 479 us; the launch traced here: 477 us
  waiting for transfers between devices  228 us (48%)
  blocking collectives  115 us (24%)
  Pallas kernels  70.9 us (15%)
  starting transfers between devices  34.7 us (7%)
  between operations  14 us (3%)
  local copies, waits for them, and re-layouts  9.43 us (2%)
    all_gather x1, waiting for transfers between devices, body(): weight = lax.all_gather(column, 'dp', axis=0, tiled=False)  75.4 us
    pallas_call x1, Pallas kernels, run_layers(): pl.pallas_call(layers_kernel, grid=(2 * layers,), out_shape=(jax.ShapeDty...  70.9 us
    all_gather x1, waiting for transfers between devices, body(): column = lax.all_gather(share, 'pipe', axis=0, tiled=False)  68.8 us
    reduce_scatter x1, waiting for transfers between devices, body(): lax.psum_scatter(terms.astype(BF16).reshape(features, 4 * HEAD), 'dp', sc...  60.8 us
    all_to_all x1, blocking collectives, body(): lax.all_to_all(packed.reshape(2, sections, ROWS, features), 'pipe', split...  51.5 us
    all_gather x1, blocking collectives, body(): gains = lax.all_gather(gain, 'pipe', axis=0, tiled=False)  25.2 us
    all_to_all x1, blocking collectives, body(): lax.all_to_all(grads.reshape(sections, ROWS, columns), 'pipe', split_axis...  23.9 us
    all_to_all x1, starting transfers between devices, body(): lax.all_to_all(outgoing, 'dp', split_axis=0, concat_axis=0, tiled=True)  17 us
  transfers between devices with their start and end apart: 6, of which 5 were waited for; matrix products, arithmetic and copies ran while one was open for 1% of the time, Pallas kernels for 0%

profile of v1, /device:TPU:1, one launch (start us, length us, event | category | flops | bytes accessed | tf_op | source)
XLA Modules:
  0.0 476.5 jit_solution(365580080047947554)
XLA Ops:
  7.3 1.5 fusion.3
  8.9 68.8 %all-gather.7.cloned.1.call-done = bf16[32,64,256]{2,1,0:T(8,128)(2,1)} async-done(((bf16[2,64,256]{2,1,0:T(8,128)(2,1)}), bf16[32,64,256]{2,1,0:T(8,128)(2,1)}) %all-gather.7.cloned.1.call-update) | async-done | bytes 1048592 | tf_op jit(solution)/shard_map/all_gather | solution.py:206
  77.7 0.1 copy.54
  77.8 0.1 copy.55
  77.9 0.1 reduce_sum.22
  77.9 0.1 mul.34
  78.0 0.1 copy.53
  78.1 0.1 eq.62
  78.2 0.1 copy.56
  78.4 0.1 copy.68
  78.5 0.1 fusion
  78.6 0.5 broadcast.195
  79.1 0.7 reduce.2
  79.8 0.7 reshape.228
  80.5 17.0 %all-to-all-start = ((bf16[32,2,320]{2,1,0:T(2,128)(2,1)}), bf16[32,2,320]{2,1,0:T(2,128)(2,1)S(1)}, u32[]{:S(2)}, u32[]{:S(2)}) async-start(bf16[32,2,320]{2,1,0:T(2,128)(2,1)} %reshape.228), calls=%async_computation | async-start | bytes 98304 | tf_op jit(solution)/shard_map/all_to_all | solution.py:220
  97.6 25.2 %all-gather.3 = f32[16,2,2048]{2,1,0:T(2,128)S(1)} all-gather(f32[1,2,2048]{2,1,0:T(2,128)S(1)} %bitcast.80), channel_id=2, replica_groups=mesh['pipe'=16,'dp'=32] {'pipe'}, dimensions={0}, use_global_device_ids=true | all-gather | bytes 278528 | tf_op jit(solution)/shard_map/all_gather | solution.py:208
  122.8 0.2 copy.59
  123.0 0.1 reshape.229
  123.1 0.2 convert_reduce_fusion
  123.3 0.1 convolution_convert_fusion
  123.5 0.1 reshape.216
  123.5 0.6 reshape.199
  124.2 5.6 %all-to-all-start.1 = ((bf16[16,8,128]{2,1,0:T(8,128)(2,1)}), bf16[16,8,128]{2,1,0:T(8,128)(2,1)S(1)}, u32[]{:S(2)}, u32[]{:S(2)}) async-start(bf16[16,8,128]{2,1,0:T(8,128)(2,1)} %reshape.199), calls=%async_computation.1 | async-start | bytes 65536 | tf_op jit(solution)/shard_map/all_to_all | solution.py:229
  129.9 0.1 fusion.16
  130.0 0.1 and_select_fusion
  130.1 0.1 tile.10.bias_ref
  130.2 0.1 pad_maximum_fusion
  130.2 11.0 %all-to-all-done.1 = bf16[16,8,128]{2,1,0:T(8,128)(2,1)S(1)} async-done(((bf16[16,8,128]{2,1,0:T(8,128)(2,1)}), bf16[16,8,128]{2,1,0:T(8,128)(2,1)S(1)}, u32[]{:S(2)}, u32[]{:S(2)}) %all-to-all-start.1) | async-done | bytes 32800 | tf_op jit(solution)/shard_map/all_to_all | solution.py:229
  141.3 75.4 %all-gather.9.cloned.1.call-done = bf16[512,2,64,256]{3,2,1,0:T(8,128)(2,1)} async-done(((bf16[16,2,64,256]{3,2,1,0:T(8,128)(2,1)}), bf16[512,2,64,256]{3,2,1,0:T(8,128)(2,1)}) %all-gather.9.cloned.1.call-update) | async-done | bytes 33554448 | tf_op jit(solution)/shard_map/all_gather | solution.py:207
  216.7 70.9 %shard_map.94 = (bf16[32,8,2048]{2,1,0:T(8,128)(2,1)S(1)}, bf16[32,8,256]{2,1,0:T(8,128)(2,1)S(1)}, bf16[128,128]{1,0:T(8,128)(2,1)S(1)}) custom-call(bf16[128,128]{1,0:T(8,128)(2,1)S(1)} %bitcast.66, bf16[128,128]{1,0:T(8,128)(2,1)S(1)} %dynamic-slice_bitcast_fusion.last_ref, f32[8,128]{1,0:T(8,128)S(1)} %get-tuple-element.32.cos_ref, ...), custom_call_target="tpu_custom_call" | custom-call | tf_op jit(solution)/shard_map/pallas_call | solution.py:154
  287.6 0.7 copy.61
  288.2 12.0 %all-to-all-start.4 = ((bf16[2,16,8,256]{3,2,0,1:T(8,128)(2,1)}), bf16[2,16,8,256]{3,2,0,1:T(8,128)(2,1)S(1)}, u32[]{:S(2)}, u32[]{:S(2)}) async-start(bf16[2,16,8,256]{3,2,0,1:T(8,128)(2,1)} %copy.61), calls=%async_computation.4 | async-start | bytes 262144 | tf_op jit(solution)/shard_map/all_to_all | solution.py:250
  300.3 0.1 copy.62
  300.4 12.0 %all-to-all-done.4 = bf16[2,16,8,256]{3,2,0,1:T(8,128)(2,1)S(1)} async-done(((bf16[2,16,8,256]{3,2,0,1:T(8,128)(2,1)}), bf16[2,16,8,256]{3,2,0,1:T(8,128)(2,1)S(1)}, u32[]{:S(2)}, u32[]{:S(2)}) %all-to-all-start.4) | async-done | bytes 131104 | tf_op jit(solution)/shard_map/all_to_all | solution.py:250
  312.4 51.5 %all_to_all.44 = bf16[2,16,8,2048]{3,2,0,1:T(8,128)(2,1)S(1)} all-to-all(bf16[2,16,8,2048]{3,2,0,1:T(8,128)(2,1)S(1)} %copy.62), channel_id=1, replica_groups=mesh['pipe'=16,'dp'=32] {'pipe'}, dimensions={1} | all-to-all | bytes 2097152 | tf_op jit(solution)/shard_map/all_to_all | solution.py:247
  363.9 0.7 bitcast_convert_fusion
  364.7 2.5 copy.63
  367.2 23.9 %all_to_all.45 = bf16[16,8,128]{2,1,0:T(8,128)(2,1)S(1)} all-to-all(bf16[16,8,128]{2,1,0:T(8,128)(2,1)S(1)} %bitcast.68), channel_id=1, replica_groups=mesh['pipe'=16,'dp'=32] {'pipe'}, dimensions={0} | all-to-all | bytes 65536 | tf_op jit(solution)/shard_map/all_to_all | solution.py:239
  391.2 0.2 fusion.1
  391.4 0.7 reduce.3
  392.1 14.0 %all_to_all.46 = bf16[32,2,256]{2,1,0:T(2,128)(2,1)S(1)} all-to-all(bf16[32,2,256]{2,1,0:T(2,128)(2,1)S(1)} %reshape.230), channel_id=1, replica_groups=mesh['pipe'=16,'dp'=32] {'dp'}, dimensions={0} | all-to-all | bytes 65536 | tf_op jit(solution)/shard_map/all_to_all | solution.py:244
  406.1 0.2 convolution_convert_fusion.2
  406.3 0.6 reshape.208
  406.9 60.8 %reduce-scatter.2.cloned.1.call-done = bf16[64,512]{1,0:T(8,128)(2,1)} async-done(((bf16[2048,512]{1,0:T(8,128)(2,1)}), bf16[64,512]{1,0:T(8,128)(2,1)}) %reduce-scatter.2.cloned.1.call-update) | async-done | bytes 65552 | tf_op jit(solution)/shard_map/reduce_scatter | solution.py:254
  467.7 0.9 reshape.218
  468.6 0.1 fusion.23
  468.7 0.6 copy.65
  469.4 0.6 copy.64
  (41 shorter events, 0.6 us)
Async XLA Ops:
  7.2 90.4 %copy-start = (bf16[128,2048]{1,0:T(8,128)(2,1)S(1)}, bf16[128,2048]{1,0:T(8,128)(2,1)}, u32[]{:S(2)}) copy-start(bf16[128,2048]{1,0:T(8,128)(2,1)} %param.13) | copy-start | bytes 1572868
  7.2 70.5 %copy-start.3 = (s32[16,4]{0,1:T(4,128)S(1)}, s32[16,4]{0,1:T(4,128)}, u32[]{:S(2)}) copy-start(s32[16,4]{0,1:T(4,128)} %param.8) | copy-start | bytes 772
  7.2 70.8 %copy-start.4 = (s32[16,2]{0,1:T(2,128)S(1)}, s32[16,2]{0,1:T(2,128)}, u32[]{:S(2)}) copy-start(s32[16,2]{0,1:T(2,128)} %param.9) | copy-start | bytes 388
  7.2 71.3 %copy-start.1 = (bf16[128,128]{1,0:T(8,128)(2,1)S(1)}, bf16[128,128]{1,0:T(8,128)(2,1)}, u32[]{:S(2)}) copy-start(bf16[128,128]{1,0:T(8,128)(2,1)} %param.7) | copy-start | bytes 98308
  7.2 90.3 %copy-start.2 = (f32[2,2048]{1,0:T(2,128)S(1)}, f32[2,2048]{1,0:T(2,128)}, u32[]{:S(2)}) copy-start(f32[2,2048]{1,0:T(2,128)} %param.10) | copy-start | bytes 49156
  7.2 70.4 %all-gather.7.cloned.1.call-start = ((), (), s32[]{:S(2)}) async-start(), calls=%async_computation.8 | async-start | bytes 1114112 | tf_op jit(solution)/shard_map/all_gather | solution.py:206
  8.8 207.9 %all-gather.9.cloned.1.call-start = ((), (), s32[]{:S(2)}) async-start(), calls=%async_computation.9 | async-start | bytes 34603008 | tf_op jit(solution)/shard_map/all_gather | solution.py:207
  80.5 42.4 %all-to-all-start = ((bf16[32,2,320]{2,1,0:T(2,128)(2,1)}), bf16[32,2,320]{2,1,0:T(2,128)(2,1)S(1)}, u32[]{:S(2)}, u32[]{:S(2)}) async-start(bf16[32,2,320]{2,1,0:T(2,128)(2,1)} %reshape.228), calls=%async_computation | async-start | bytes 98304 | tf_op jit(solution)/shard_map/all_to_all | solution.py:220
  124.2 17.1 %all-to-all-start.1 = ((bf16[16,8,128]{2,1,0:T(8,128)(2,1)}), bf16[16,8,128]{2,1,0:T(8,128)(2,1)S(1)}, u32[]{:S(2)}, u32[]{:S(2)}) async-start(bf16[16,8,128]{2,1,0:T(8,128)(2,1)} %reshape.199), calls=%async_computation.1 | async-start | bytes 65536 | tf_op jit(solution)/shard_map/all_to_all | solution.py:229
  288.2 24.2 %all-to-all-start.4 = ((bf16[2,16,8,256]{3,2,0,1:T(8,128)(2,1)}), bf16[2,16,8,256]{3,2,0,1:T(8,128)(2,1)S(1)}, u32[]{:S(2)}, u32[]{:S(2)}) async-start(bf16[2,16,8,256]{3,2,0,1:T(8,128)(2,1)} %copy.61), calls=%async_computation.4 | async-start | bytes 262144 | tf_op jit(solution)/shard_map/all_to_all | solution.py:250
  300.3 167.4 %reduce-scatter.2.cloned.1.call-start = ((), (), s32[]{:S(2)}) async-start(), calls=%async_computation.7 | async-start | bytes 2162688 | tf_op jit(solution)/shard_map/reduce_scatter | solution.py:254
Sparse Core Ops, SparseCore 0:
  10.7 66.8 all-gather.6
  80.8 135.8 all-gather.8
  367.3 100.3 reduce-scatter.1

commit v2 on v1

v2 whole, which is shorter than its diff:
```python
import jax
import jax.numpy as jnp
from jax import lax
from jax.experimental import pallas as pl
from jax.experimental.pallas import tpu as pltpu
from jax.sharding import PartitionSpec as P

ROPE_BASE = 500000.0
EPSILON = 1e-05
NEGATIVE = -1e30
HEADS = 16
ROWS = 8
HEAD = 128
SECTIONS = 16
GROUPS = 32
LAYERS = 32
SIDE = 4
PART = 64
TILE = HEADS * ROWS
FEATURES = HEADS * HEAD
F32 = jnp.float32
BF16 = jnp.bfloat16
MESH = pl.DeviceIdType.MESH


def document_positions(lengths, row_count):
    doc_ends = jnp.cumsum(lengths, axis=-1)
    doc_starts = doc_ends - lengths
    row_numbers = jnp.arange(row_count, dtype=jnp.int32)
    document = jnp.sum(
        (row_numbers[None, :, None] >= doc_ends[:, None, :-1]).astype(jnp.int32),
        axis=-1,
        dtype=jnp.int32,
    )
    picked = document[:, :, None] == jnp.arange(lengths.shape[1], dtype=jnp.int32)[None, None, :]
    opening = jnp.sum(jnp.where(picked, doc_starts[:, None, :], 0), axis=-1, dtype=jnp.int32)
    return (document, row_numbers[None, :] - opening)


def dot(a, b, over_a, over_b):
    return lax.dot_general(
        a, b, (((over_a,), (over_b,)), ((), ())), preferred_element_type=F32
    )


def swap_halves(flat):
    return pltpu.roll(flat, HEAD // 2, 1)


def turn(flat, cosine, sine):
    return flat * cosine + swap_halves(flat) * sine


def unturn(flat, cosine, sine):
    return flat * cosine - swap_halves(flat) * sine


def side_by_side(flat):
    return jnp.concatenate([flat[ROWS * h:ROWS * (h + 1)] for h in range(HEADS)], axis=1)


def stacked(wide):
    return jnp.concatenate([wide[:, HEAD * h:HEAD * (h + 1)] for h in range(HEADS)], axis=0)


def row_mean(flat):
    total = jnp.sum(flat.reshape(HEADS, ROWS, HEAD), axis=0)
    return jnp.sum(total, axis=-1, keepdims=True) * (1.0 / (HEADS * HEAD))


def over_heads(rows):
    return jnp.broadcast_to(rows[None], (HEADS, ROWS, rows.shape[-1])).reshape(
        HEADS * ROWS, rows.shape[-1]
    )


def gain_rows(gain):
    return jnp.broadcast_to(gain[:, None, :], (HEADS, ROWS, HEAD)).reshape(HEADS * ROWS, HEAD)


def whole_kernel(
    source_ref, lane_route_ref, last_ref, cos_ref, sin_ref, gain_ref, key_ref, value_ref,
    grad_ref, key_out_ref, value_out_ref,
    weight, gains, current, saved, saved_queries, saved_keys, saved_weights, saved_scale, bias, turns,
    packed_all, packed_in, pairs_all, pairs_in, terms, twin_in, chip_terms, chip_in,
    sorting, placing, half_out, half_in, rows_out, rows_in, back_out, back_in, home_out, home_in,
    own_sem, zw_recv, zw_right, zw_left, zg_recv, zg_right, zg_left,
    ring_send, ring_recv, packed_send, packed_recv, pair_send, pair_recv,
    half_send, half_recv, rows_send, rows_recv, back_send, back_recv, home_send, home_recv,
    twin_send, twin_recv, chip_send, chip_recv,
):
    z = lax.axis_index("pipe")
    d = lax.axis_index("dp")
    core = d % 2
    chip = d // 2
    px, py = chip // SIDE, chip % SIDE
    twin = chip * 2 + 1 - core
    z_next, z_before = (z + 1) % SECTIONS, (z + SECTIONS - 1) % SECTIONS

    def remote(src, dst, send, recv, to_z, to_d):
        return pltpu.make_async_remote_copy(
            src_ref=src, dst_ref=dst, send_sem=send, recv_sem=recv,
            device_id={"pipe": to_z, "dp": to_d}, device_id_type=MESH,
        )

    def await_recv(ref, sem):
        remote(ref, ref, sem, sem, z, twin).wait_recv()

    def await_send(ref, sem):
        remote(ref, ref, sem, sem, z, twin).wait_send()

    def loop(low, high, run):
        lax.fori_loop(low, high, lambda i, c: (run(i), c)[1], 0)

    owned = []
    for v in range(2):
        layer = v * SECTIONS + z
        rows = pl.ds(pl.multiple_of(d * PART, PART), PART)
        own = weight.at[layer, px, py, core]
        owned.append(pltpu.make_async_copy(
            key_ref.at[v, rows, :], own.at[:, pl.ds(0, HEAD)], own_sem.at[v, 0]))
        owned.append(pltpu.make_async_copy(
            value_ref.at[v, rows, :], own.at[:, pl.ds(HEAD, HEAD)], own_sem.at[v, 1]))
    for copy in owned:
        copy.start()
    for v in range(2):
        gains[v * SECTIONS + z] = gain_ref[v]

    row = lax.broadcasted_iota(jnp.int32, (2 * TILE, 2 * TILE), 0)
    col = lax.broadcasted_iota(jnp.int32, (2 * TILE, 2 * TILE), 1)
    kind_row = (col // TILE) * (ROWS // 2) + col % (ROWS // 2)
    sort = jnp.where((lane_route_ref[...] == row // ROWS) & (row % ROWS == kind_row), 1.0, 0.0)
    sort = sort.astype(BF16)
    sorting[...] = sort[:, :TILE]
    half_out[...] = dot(sort, source_ref[...], 1, 0).reshape(GROUPS, ROWS, HEAD)
    half_in[d] = half_out[d]

    barrier = pltpu.get_barrier_semaphore()

    def greet_plane(k):
        pl.semaphore_signal(
            barrier, inc=1, device_id={"pipe": z, "dp": (d + k) % GROUPS}, device_id_type=MESH)

    def greet_line(k):
        pl.semaphore_signal(
            barrier, inc=1, device_id={"pipe": (z + k) % SECTIONS, "dp": d}, device_id_type=MESH)

    loop(1, GROUPS, greet_plane)
    loop(1, SECTIONS, greet_line)
    pl.semaphore_wait(barrier, GROUPS + SECTIONS - 2)

    def send_half(k):
        to = (d + k) % GROUPS
        remote(half_out.at[to], half_in.at[d], half_send.at[to], half_recv.at[d], z, to).start()

    for copy in owned:
        copy.wait()

    def line_step(v, s):
        from_left = v * SECTIONS + (z + SECTIONS - s) % SECTIONS
        from_right = v * SECTIONS + (z + s) % SECTIONS

        @pl.when(s >= 1)
        def _():
            await_recv(weight.at[from_left, px, py, core], zw_recv.at[from_left])
            await_recv(gains.at[from_left], zg_recv.at[from_left])

        @pl.when(s <= 7)
        def _():
            own = weight.at[from_left, px, py, core]
            remote(own, own, zw_right.at[v, s], zw_recv.at[from_left], z_next, d).start()
            line = gains.at[from_left]
            remote(line, line, zg_right.at[v, s], zg_recv.at[from_left], z_next, d).start()

        @pl.when((s >= 1) & (s <= 7))
        def _():
            await_recv(weight.at[from_right, px, py, core], zw_recv.at[from_right])
            await_recv(gains.at[from_right], zg_recv.at[from_right])

        @pl.when(s <= 6)
        def _():
            own = weight.at[from_right, px, py, core]
            remote(own, own, zw_left.at[v, s], zw_recv.at[from_right], z_before, d).start()
            line = gains.at[from_right]
            remote(line, line, zg_left.at[v, s], zg_recv.at[from_right], z_before, d).start()

    line_step(0, 0)
    loop(1, GROUPS, send_half)
    loop(1, 4, lambda s: line_step(0, s))

    def await_half(k):
        at = (d + k) % GROUPS
        await_recv(half_in.at[at], half_recv.at[at])

    loop(1, GROUPS, await_half)
    arrived = half_in[...]
    slot = jnp.broadcast_to(arrived[:, 4:5, HEAD // 2:HEAD // 2 + 1], (GROUPS, ROWS, 1))
    slot = slot.reshape(2 * TILE, 1)
    arrived = arrived.reshape(2 * TILE, HEAD).astype(BF16)
    row = lax.broadcasted_iota(jnp.int32, (2 * TILE, TILE), 0) % ROWS
    col = lax.broadcasted_iota(jnp.int32, (2 * TILE, TILE), 1)
    same = slot == (col // (ROWS // 2)).astype(F32)
    place = jnp.where(same & (row == col % (ROWS // 2)), 1.0, 0.0).astype(BF16)
    place_tags = jnp.where(same & (row == col % (ROWS // 2) + ROWS // 2), 1.0, 0.0).astype(BF16)
    placing[...] = place
    rows_out[...] = dot(place, arrived, 0, 0).reshape(SECTIONS, ROWS, HEAD)
    home_out[pl.ds(0, SECTIONS)] = dot(place_tags, arrived, 0, 0).reshape(SECTIONS, ROWS, HEAD)
    rows_in[z] = rows_out[z]

    def send_rows(k):
        to = (z + k) % SECTIONS
        remote(rows_out.at[to], rows_in.at[z], rows_send.at[to], rows_recv.at[z], to, d).start()

    loop(1, SECTIONS, send_rows)

    tags = home_out[z]
    document = jnp.broadcast_to(tags[:, 0:1], (ROWS, TILE))
    position = jnp.broadcast_to(tags[:, HEAD // 4:HEAD // 4 + 1], (ROWS, TILE))
    lane = lax.broadcasted_iota(jnp.int32, (ROWS, TILE), 1) % ROWS
    mine = lane == lax.broadcasted_iota(jnp.int32, (ROWS, TILE), 0)
    query_document = jnp.sum(jnp.where(mine, document, 0.0), axis=0, keepdims=True)
    query_position = jnp.sum(jnp.where(mine, position, 0.0), axis=0, keepdims=True)
    allowed = (document == query_document) & (position <= query_position)
    bias[...] = jnp.where(allowed, 0.0, NEGATIVE)
    cosine = jnp.zeros((ROWS, HEAD), F32)
    sine = jnp.zeros((ROWS, HEAD), F32)
    for p in range(ROWS):
        cosine = jnp.where(position == float(p), cos_ref[p:p + 1, :], cosine)
        sine = jnp.where(position == float(p), sin_ref[p:p + 1, :], sine)
    turns[0] = cosine
    turns[1] = sine

    loop(4, 9, lambda s: line_step(0, s))

    def await_rows(k):
        at = (z + k) % SECTIONS
        await_recv(rows_in.at[at], rows_recv.at[at])

    loop(1, SECTIONS, await_rows)
    current[...] = rows_in[...].reshape(TILE, HEAD)

    def forward(layer):
        cosine, sine = turns[0], turns[1]
        cosine_all, sine_all = over_heads(cosine), over_heads(sine)
        x = current[...]
        saved[layer] = x
        scale = lax.rsqrt(row_mean(x * x) + EPSILON)
        saved_scale[layer] = scale
        normed = x * over_heads(scale) * gain_rows(gains[layer])
        wide = side_by_side(normed)
        pre = dot(wide.astype(BF16), weight[layer].reshape(FEATURES, 2 * HEAD), 1, 0)
        packed = jnp.concatenate(
            [wide[:, :FEATURES // 2], wide[:, FEATURES // 2:]], axis=0).astype(BF16)
        packed_all[layer] = packed
        owner, v = layer % SECTIONS, layer // SECTIONS

        @pl.when(owner != z)
        def _():
            remote(packed_all.at[layer], packed_in.at[v, z],
                   packed_send.at[layer], packed_recv.at[v, z], owner, d).start()

        @pl.when(owner == z)
        def _():
            packed_in[v, z] = packed

        keys = turn(pre[:, :HEAD], cosine, sine).astype(BF16)
        values = pre[:, HEAD:].astype(BF16)
        queries = turn(normed, cosine_all, sine_all).astype(BF16)
        scores = dot(keys, queries, 1, 1) * HEAD ** (-0.5) + bias[...]
        raised = jnp.exp(scores - jnp.max(scores, axis=0, keepdims=True))
        weights = raised / jnp.sum(raised, axis=0, keepdims=True)
        saved_queries[layer] = queries
        saved_keys[layer, 0] = keys
        saved_keys[layer, 1] = values
        saved_weights[layer] = weights
        current[...] = x + dot(weights.astype(BF16), values, 0, 0)

    def plane(layer, e, at_first, at_second, rows):
        if e == 0:
            first = px if at_first is None else at_first
            second = py if at_second is None else at_second
            if at_first is all:
                return weight.at[layer, :, second, core, rows, :]
            return weight.at[layer, first, second, core, rows, :]
        first = py if at_first is None else at_first
        second = px if at_second is None else at_second
        if at_first is all:
            return weight.at[layer, second, :, core, rows, :]
        return weight.at[layer, second, first, core, rows, :]

    def device_of(e, along_first, along_second):
        dx, dy = (along_first, along_second) if e == 0 else (along_second, along_first)
        return (((px + dx) % SIDE) * SIDE + (py + dy) % SIDE) * 2 + core

    every, low, high = pl.ds(0, PART), pl.ds(0, PART // 2), pl.ds(PART // 2, PART // 2)

    def around(e, which, by):
        base = (px if which == 0 else py) if e == 0 else (py if which == 0 else px)
        return (base + by) % SIDE

    def stage_one(layer, e):
        own = plane(layer, e, None, None, every)
        remote(own, own, ring_send.at[layer, 0], ring_recv.at[layer, 0], z, device_of(e, 1, 0)).start()
        remote(own, own, ring_send.at[layer, 0], ring_recv.at[layer, 1], z, device_of(e, 3, 0)).start()

    def stage_two(layer, e):
        left, right = around(e, 0, 3), around(e, 0, 1)
        await_recv(plane(layer, e, left, None, every), ring_recv.at[layer, 0])
        part = plane(layer, e, left, None, low)
        remote(part, part, ring_send.at[layer, 1], ring_recv.at[layer, 2], z, device_of(e, 1, 0)).start()
        await_recv(plane(layer, e, right, None, every), ring_recv.at[layer, 1])
        part = plane(layer, e, right, None, high)
        remote(part, part, ring_send.at[layer, 1], ring_recv.at[layer, 3], z, device_of(e, 3, 0)).start()

    def stage_three(layer, e):
        far = around(e, 0, 2)
        await_recv(plane(layer, e, far, None, low), ring_recv.at[layer, 2])
        await_recv(plane(layer, e, far, None, high), ring_recv.at[layer, 3])
        line = plane(layer, e, all, None, every)
        remote(line, line, ring_send.at[layer, 2], ring_recv.at[layer, 4], z, device_of(e, 0, 1)).start()
        remote(line, line, ring_send.at[layer, 2], ring_recv.at[layer, 5], z, device_of(e, 0, 3)).start()

    def stage_four(layer, e):
        left, right = around(e, 1, 3), around(e, 1, 1)
        await_recv(plane(layer, e, all, left, every), ring_recv.at[layer, 4])
        part = plane(layer, e, all, left, low)
        remote(part, part, ring_send.at[layer, 3], ring_recv.at[layer, 6], z, device_of(e, 0, 1)).start()
        await_recv(plane(layer, e, all, right, every), ring_recv.at[layer, 5])
        part = plane(layer, e, all, right, high)
        remote(part, part, ring_send.at[layer, 3], ring_recv.at[layer, 7], z, device_of(e, 0, 3)).start()

    def stage_five(layer, e):
        far = around(e, 1, 2)
        await_recv(plane(layer, e, all, far, low), ring_recv.at[layer, 6])
        await_recv(plane(layer, e, all, far, high), ring_recv.at[layer, 7])
        half = weight.at[layer, :, :, core]
        remote(half, half, ring_send.at[layer, 4], ring_recv.at[layer, 8], z, twin).start()

    def stage_six(layer, e):
        await_recv(weight.at[layer, :, :, 1 - core], ring_recv.at[layer, 8])
        forward(layer)

    stages = ((4, stage_five), (3, stage_four), (2, stage_three), (1, stage_two), (0, stage_one),
              (5, stage_six))
    pairs = LAYERS // 2

    def turn_of(t):
        @pl.when(t <= 8)
        def _():
            line_step(1, t)

        for late, stage in stages:
            @pl.when((t >= late) & (t < late + pairs))
            def _():
                for e in range(2):
                    stage(2 * (t - late) + e, e)

    loop(0, pairs + 5, turn_of)

    current[...] = last_ref[...]

    def backward(step):
        layer = LAYERS - 1 - step
        cosine, sine = turns[0], turns[1]
        cosine_all, sine_all = over_heads(cosine), over_heads(sine)
        upstream = current[...]
        rounded = upstream.astype(BF16)
        keys = saved_keys[layer, 0]
        values = saved_keys[layer, 1]
        weights = saved_weights[layer]
        d_weights = dot(values, rounded, 1, 1).astype(BF16).astype(F32)
        d_values = dot(weights.astype(BF16), rounded, 1, 0).astype(BF16).astype(F32)
        inner = jnp.sum(d_weights * weights, axis=0, keepdims=True)
        d_scores = (weights * (d_weights - inner) * HEAD ** (-0.5)).astype(BF16)
        d_queries = dot(d_scores, keys, 0, 0).astype(BF16).astype(F32)
        d_keys = dot(d_scores, saved_queries[layer], 1, 0).astype(BF16).astype(F32)
        d_key_pre = unturn(d_keys, cosine, sine)
        pair = jnp.concatenate([d_key_pre, d_values], axis=1)
        pairs_all[layer] = pair
        owner, v = layer % SECTIONS, layer // SECTIONS

        @pl.when(owner != z)
        def _():
            remote(pairs_all.at[layer], pairs_in.at[v, z],
                   pair_send.at[layer], pair_recv.at[v, z], owner, d).start()

        @pl.when(owner == z)
        def _():
            pairs_in[v, z] = pair

        d_packed = stacked(
            dot(pair.astype(BF16), weight[layer].reshape(FEATURES, 2 * HEAD), 1, 1))
        d_normed = unturn(d_queries, cosine_all, sine_all) + d_packed
        x = saved[layer]
        scale = saved_scale[layer]
        scaled = d_normed * gain_rows(gains[layer])
        pull = row_mean(scaled * x) * scale * scale * scale
        current[...] = upstream + scaled * over_heads(scale) - x * over_heads(pull)

    loop(0, LAYERS, backward)

    back_out[...] = current[...].astype(BF16).astype(F32).reshape(SECTIONS, ROWS, HEAD)
    back_in[z] = back_out[z]

    def send_back(k):
        to = (z + k) % SECTIONS
        remote(back_out.at[to], back_in.at[z], back_send.at[to], back_recv.at[z], to, d).start()

    loop(1, SECTIONS, send_back)

    for v in range(2):
        def await_rows_of(k):
            at = (z + k) % SECTIONS
            await_recv(packed_in.at[v, at], packed_recv.at[v, at])
            await_recv(pairs_in.at[v, at], pair_recv.at[v, at])

        loop(1, SECTIONS, await_rows_of)
        pair = pairs_in[v]
        nothing = jnp.zeros_like(pair)
        upper = jnp.concatenate([pair, nothing], axis=1).reshape(2 * TILE, 2 * HEAD)
        lower = jnp.concatenate([nothing, pair], axis=1).reshape(2 * TILE, 2 * HEAD)
        both = jnp.concatenate([upper, lower], axis=1).astype(BF16)
        product = dot(packed_in[v].reshape(2 * TILE, FEATURES // 2), both, 0, 0).astype(BF16)
        for g in range(GROUPS):
            rows = product[PART * (g % 16):PART * (g % 16 + 1)]
            terms[g // 2, g % 2, v] = rows[:, 2 * HEAD * (g // 16):2 * HEAD * (g // 16 + 1)]

    across = remote(terms.at[:, 1 - core], twin_in, twin_send, twin_recv, z, twin)
    across.start()

    def await_back(k):
        at = (z + k) % SECTIONS
        await_recv(back_in.at[at], back_recv.at[at])

    loop(1, SECTIONS, await_back)
    mine = back_in[...].reshape(TILE, HEAD).astype(BF16)
    home_out[...] = dot(placing[...], mine, 1, 0).reshape(GROUPS, ROWS, HEAD)
    home_in[d] = home_out[d]

    def send_home(k):
        to = (d + k) % GROUPS
        remote(home_out.at[to], home_in.at[d], home_send.at[to], home_recv.at[d], z, to).start()

    loop(1, GROUPS, send_home)

    across.wait()
    chip_terms[...] = (terms[:, core].astype(F32) + twin_in[...].astype(F32)).astype(BF16)

    def send_chip(k):
        to = (chip + k) % (GROUPS // 2)
        remote(chip_terms.at[to], chip_in.at[chip], chip_send.at[to], chip_recv.at[chip],
               z, 2 * to + core).start()

    loop(1, GROUPS // 2, send_chip)
    chip_in[chip] = chip_terms[chip]

    def await_home(k):
        at = (d + k) % GROUPS
        await_recv(home_in.at[at], home_recv.at[at])

    loop(1, GROUPS, await_home)
    arrived = home_in[...].reshape(2 * TILE, HEAD).astype(BF16)
    grad_ref[...] = dot(sorting[...], arrived, 0, 0).astype(BF16)

    def sent_layer(layer):
        await_send(weight.at[layer, pl.ds(0, 2), 0, 0], ring_send.at[layer, 0])
        await_send(weight.at[layer, 0, 0, 0], ring_send.at[layer, 1])
        await_send(weight.at[layer, pl.ds(0, 2), :, 0], ring_send.at[layer, 2])
        await_send(weight.at[layer, 0, :, 0], ring_send.at[layer, 3])
        await_send(weight.at[layer, :, :, 0], ring_send.at[layer, 4])

        @pl.when(layer % SECTIONS != z)
        def _():
            await_send(packed_all.at[layer], packed_send.at[layer])
            await_send(pairs_all.at[layer], pair_send.at[layer])

    loop(0, LAYERS, sent_layer)
    for v in range(2):
        def sent_line(s):
            await_send(weight.at[0, 0, 0, 0], zw_right.at[v, s])
            await_send(gains.at[0], zg_right.at[v, s])

            @pl.when(s <= 6)
            def _():
                await_send(weight.at[0, 0, 0, 0], zw_left.at[v, s])
                await_send(gains.at[0], zg_left.at[v, s])

        loop(0, 8, sent_line)

    def sent_plane(k):
        to = (d + k) % GROUPS
        await_send(half_out.at[to], half_send.at[to])
        await_send(home_out.at[to], home_send.at[to])

    def sent_sections(k):
        to = (z + k) % SECTIONS
        await_send(rows_out.at[to], rows_send.at[to])
        await_send(back_out.at[to], back_send.at[to])

    loop(1, GROUPS, sent_plane)
    loop(1, SECTIONS, sent_sections)

    def await_chip(k):
        at = (chip + k) % (GROUPS // 2)
        await_recv(chip_in.at[at], chip_recv.at[at])
        to = (chip + k) % (GROUPS // 2)
        await_send(chip_terms.at[to], chip_send.at[to])

    loop(1, GROUPS // 2, await_chip)
    for v in range(2):
        total = jnp.zeros((PART, 2 * HEAD), F32)
        for k in range(GROUPS // 2):
            total = total + chip_in[k, v].astype(F32)
        key_out_ref[v] = total[:, :HEAD]
        value_out_ref[v] = total[:, HEAD:]


def run_whole(source, lane_route, last, cosine, sine, gain, key_weight, value_weight):
    whole = pl.BlockSpec(memory_space=pltpu.VMEM)
    remote = pl.BlockSpec(memory_space=pl.ANY)
    dma = pltpu.SemaphoreType.DMA
    small = pltpu.VMEM((SECTIONS, ROWS, HEAD), F32)
    large = pltpu.VMEM((GROUPS, ROWS, HEAD), F32)
    chips = GROUPS // 2
    return pl.pallas_call(
        whole_kernel,
        out_shape=(
            jax.ShapeDtypeStruct((TILE, HEAD), BF16),
            jax.ShapeDtypeStruct((2, PART, HEAD), F32),
            jax.ShapeDtypeStruct((2, PART, HEAD), F32),
        ),
        in_specs=[whole] * 6 + [remote] * 2,
        out_specs=(whole, whole, whole),
        scratch_shapes=[
            pltpu.VMEM((LAYERS, SIDE, SIDE, 2, PART, 2 * HEAD), BF16),
            pltpu.VMEM((LAYERS, HEADS, HEAD), F32),
            pltpu.VMEM((TILE, HEAD), F32),
            pltpu.VMEM((LAYERS, TILE, HEAD), F32),
            pltpu.VMEM((LAYERS, TILE, HEAD), BF16),
            pltpu.VMEM((LAYERS, 2, ROWS, HEAD), BF16),
            pltpu.VMEM((LAYERS, ROWS, TILE), F32),
            pltpu.VMEM((LAYERS, ROWS, 1), F32),
            pltpu.VMEM((ROWS, TILE), F32),
            pltpu.VMEM((2, ROWS, HEAD), F32),
            pltpu.VMEM((LAYERS, 2 * ROWS, FEATURES // 2), BF16),
            pltpu.VMEM((2, SECTIONS, 2 * ROWS, FEATURES // 2), BF16),
            pltpu.VMEM((LAYERS, ROWS, 2 * HEAD), F32),
            pltpu.VMEM((2, SECTIONS, ROWS, 2 * HEAD), F32),
            pltpu.VMEM((chips, 2, 2, PART, 2 * HEAD), BF16),
            pltpu.VMEM((chips, 2, PART, 2 * HEAD), BF16),
            pltpu.VMEM((chips, 2, PART, 2 * HEAD), BF16),
            pltpu.VMEM((chips, 2, PART, 2 * HEAD), BF16),
            pltpu.VMEM((2 * TILE, TILE), BF16),
            pltpu.VMEM((2 * TILE, TILE), BF16),
            large, large, small, small, small, small, large, large,
            dma((2, 2)),
            dma((LAYERS,)), dma((2, 8)), dma((2, 8)),
            dma((LAYERS,)), dma((2, 8)), dma((2, 8)),
            dma((LAYERS, 5)), dma((LAYERS, 9)),
            dma((LAYERS,)), dma((2, SECTIONS)), dma((LAYERS,)), dma((2, SECTIONS)),
            dma((GROUPS,)), dma((GROUPS,)), dma((SECTIONS,)), dma((SECTIONS,)),
            dma((SECTIONS,)), dma((SECTIONS,)), dma((GROUPS,)), dma((GROUPS,)),
            dma(()), dma(()), dma((chips,)), dma((chips,)),
        ],
        compiler_params=pltpu.CompilerParams(
            collective_id=0, has_side_effects=True, vmem_limit_bytes=56 * 2**20),
    )(source, lane_route, last, cosine, sine, gain, key_weight, value_weight)


def body(hidden, lengths, route, gain, key_weight, value_weight, cotangent):
    section = lax.axis_index("pipe")
    half_rows = ROWS // 2
    half_count = 2 * lengths.shape[0]

    document, position = document_positions(lengths, ROWS)
    lane = jnp.arange(HEAD, dtype=jnp.int32)[None, :]
    slot = jnp.repeat(jnp.arange(half_count, dtype=jnp.int32), half_rows)[:, None]
    tags = jnp.where(
        lane < HEAD // 4, document.reshape(TILE, 1),
        jnp.where(lane < HEAD // 2, position.reshape(TILE, 1), slot))
    source = jnp.concatenate([hidden, tags.astype(BF16)], axis=0)
    lane_route = jnp.tile(jnp.repeat(route.reshape(half_count), half_rows), 2)[None, :]
    half = HEAD // 2
    frequency = ROPE_BASE ** (-(jnp.arange(half, dtype=F32) * 2.0 / HEAD))
    angles = jnp.arange(ROWS, dtype=F32)[:, None] * frequency
    cosine, sine = jnp.cos(angles), jnp.sin(angles)
    cosine = jnp.concatenate([cosine, cosine], axis=-1)
    sine = jnp.concatenate([-sine, sine], axis=-1)
    last = lax.dynamic_slice_in_dim(cotangent, section * ROWS, ROWS, 0)
    last = jnp.swapaxes(last.reshape(ROWS, HEADS, HEAD), 0, 1).reshape(TILE, HEAD).astype(F32)
    return run_whole(
        source, lane_route, last, cosine, sine, gain.reshape(2, HEADS, HEAD),
        key_weight, value_weight)


def solution(mesh):
    placed = (
        P("dp", "pipe"),
        P("dp", None),
        P("dp", None),
        P("pipe", None),
        P("pipe", None, None),
        P("pipe", None, None),
        P("dp", None),
    )
    return jax.shard_map(
        body,
        mesh=mesh,
        in_specs=placed,
        out_specs=(P("dp", "pipe"), P("pipe", "dp", None), P("pipe", "dp", None)),
        check_vma=False,
    )
```

time: 479 us -> 249 us (0.52)
  waiting for transfers between devices: 228 us -> 0 us
  Pallas kernels: 70.9 us -> 234 us
  blocking collectives: 115 us -> 0 us
  starting transfers between devices: 34.7 us -> 0 us
  between operations: 14 us -> 0.71 us
    pallas_call x1, Pallas kernels: 70.9 us -> 234 us  [run_whole(): pl.pallas_call(whole_kernel, out_shape=(jax.ShapeDtypeStruct((TILE, HEAD)...]
    all_gather x2 -> x0, waiting for transfers between devices: 144 us -> none  [the longest x1 75.4 us: body(): weight = lax.all_gather(column, 'dp', axis=0, tiled=False)]
    all_to_all x3 -> x0, blocking collectives: 89.4 us -> none  [the longest x1 51.5 us: body(): lax.all_to_all(packed.reshape(2, sections, ROWS, features), 'pipe', split...]
    reduce_scatter x1 -> x0, waiting for transfers between devices: 60.8 us -> none  [body(): lax.psum_scatter(terms.astype(BF16).reshape(features, 4 * HEAD), 'dp', sc...]
    all_to_all x3 -> x0, starting transfers between devices: 34.6 us -> none  [the longest x1 17 us: body(): lax.all_to_all(outgoing, 'dp', split_axis=0, concat_axis=0, tiled=True)]
    all_gather x1 -> x0, blocking collectives: 25.2 us -> none  [body(): gains = lax.all_gather(gain, 'pipe', axis=0, tiled=False)]
    all_to_all x3 -> x0, waiting for transfers between devices: 23.1 us -> none  [the longest x1 12 us: body(): lax.all_to_all(pairs.reshape(2, sections, ROWS, 2 * HEAD), 'pipe', split_...]
    reshape x10 -> x1, local copies, waits for them, and re-layouts: 5.65 us -> 0.09 us  [body(): route.reshape(half_count)]
  transfers between devices with their start and end apart: 6 -> 0, of which waited for: 5 -> 0; matrix products, arithmetic and copies ran while one was open for 1% -> 0% of each run, Pallas kernels for 0% -> 0%
where the time goes in v2:
time: 249 us; the launch traced here: 244 us
  Pallas kernels  234 us (94%)
  local copies, waits for them, and re-layouts  6.61 us (3%)
  other arithmetic  2.95 us (1%)
    pallas_call x1, Pallas kernels, run_whole(): pl.pallas_call(whole_kernel, out_shape=(jax.ShapeDtypeStruct((TILE, HEAD)...  234 us
    unnamed x17, local copies, waits for them, and re-layouts  5.38 us

profile of v2, /device:TPU:1, one launch (start us, length us, event | category | flops | bytes accessed | tf_op | source)
XLA Modules:
  0.0 244.4 jit_solution(1558345608604008249)
XLA Ops:
  0.7 0.0 copy-start.4
  0.7 0.7 copy-done.4
  1.4 0.1 copy.17
  1.5 0.1 sub.21
  1.6 0.1 copy.16
  1.7 0.0 copy-start.5
  1.7 0.1 broadcast_in_dim.72
  1.7 0.6 copy-done.5
  2.3 0.1 copy.18
  2.4 0.1 reshape.54
  2.6 0.7 pad_maximum_fusion.1
  3.2 0.0 copy-start.3
  3.2 0.1 broadcast_in_dim.81
  3.3 0.1 tile.7
  3.4 0.5 tile.8
  4.0 0.0 copy-done.3
  4.0 0.6 copy.21
  4.6 0.0 copy-start.2
  4.6 0.1 broadcast_in_dim.79
  4.7 0.1 select_convert_fusion
  4.8 0.5 copy-done.2
  5.3 0.6 pad_maximum_fusion.source_ref
  6.0 1.4 convert_bitcast_fusion.last_ref
  7.4 234.1 %shard_map.94 = (bf16[128,128]{1,0:T(8,128)(2,1)}, f32[2,64,128]{2,1,0:T(8,128)}, f32[2,64,128]{2,1,0:T(8,128)}) custom-call(bf16[256,128]{1,0:T(8,128)(2,1)} %pad_maximum_fusion.source_ref, s32[1,256]{1,0:T(1,128)} %bitcast.16, f32[128,128]{1,0:T(8,128)} %convert_bitcast_fusion.last_ref, f32[8,128]{1,0:T(8,128)} %get-tuple-element.8.cos_ref, ...), custom_call_target="tpu_custom_call" | custom-call | tf_op jit(solution)/shard_map/pallas_call | solution.py:525
  241.5 0.0 copy-start.1
  241.5 1.4 copy.25
  242.9 0.0 copy-done.1
  242.9 0.0 copy-start
  242.9 0.6 copy.26
  243.6 0.2 copy-done
  243.8 0.6 copy.27
  (9 shorter events, 0.1 us)
Async XLA Ops:
  0.7 0.7 copy-start.4
  1.7 0.7 copy-start.5
  3.2 0.7 copy-start.3
  4.6 0.8 copy-start.2
  241.5 1.4 copy-start.1
  242.9 0.9 copy-start

commit v3 on v2

v3 whole, which is shorter than its diff:
```python
import math

import jax
import jax.numpy as jnp
from jax import lax
from jax.experimental import pallas as pl
from jax.experimental.pallas import tpu as pltpu
from jax.sharding import PartitionSpec as P

ROPE_BASE = 500000.0
EPSILON = 1e-05
NEGATIVE = -1e30
HEADS = 16
ROWS = 8
HEAD = 128
SECTIONS = 16
GROUPS = 32
LAYERS = 32
SIDE = 4
PART = 64
TILE = HEADS * ROWS
FEATURES = HEADS * HEAD
F32 = jnp.float32
BF16 = jnp.bfloat16
MESH = pl.DeviceIdType.MESH


def dot(a, b, over_a, over_b):
    return lax.dot_general(
        a, b, (((over_a,), (over_b,)), ((), ())), preferred_element_type=F32
    )


def swap_halves(flat):
    return pltpu.roll(flat, HEAD // 2, 1)


def turn(flat, cosine, sine):
    return flat * cosine + swap_halves(flat) * sine


def unturn(flat, cosine, sine):
    return flat * cosine - swap_halves(flat) * sine


def side_by_side(flat):
    return jnp.concatenate([flat[ROWS * h:ROWS * (h + 1)] for h in range(HEADS)], axis=1)


def stacked(wide):
    return jnp.concatenate([wide[:, HEAD * h:HEAD * (h + 1)] for h in range(HEADS)], axis=0)


def row_mean(flat):
    total = jnp.sum(flat.reshape(HEADS, ROWS, HEAD), axis=0)
    return jnp.sum(total, axis=-1, keepdims=True) * (1.0 / (HEADS * HEAD))


def over_heads(rows):
    return jnp.broadcast_to(rows[None], (HEADS, ROWS, rows.shape[-1])).reshape(
        HEADS * ROWS, rows.shape[-1]
    )


def gain_rows(gain):
    return jnp.broadcast_to(gain[:, None, :], (HEADS, ROWS, HEAD)).reshape(HEADS * ROWS, HEAD)


def whole_kernel(
    hidden_ref, lengths_ref, route_ref, gain_ref, key_ref, value_ref, cotangent_ref,
    grad_ref, key_out_ref, value_out_ref,
    weight, gains, current, saved, saved_queries, saved_keys, saved_weights, saved_scale, bias, turns,
    packed_all, packed_in, pairs_all, pairs_in, terms, twin_in, chip_terms, chip_in,
    sorting, placing, half_out, half_in, rows_out, rows_in, back_out, back_in, home_out, home_in,
    last, last_sem, own_sem, zw_recv, zw_right, zw_left, zg_recv, zg_right, zg_left,
    ring_send, ring_recv, packed_send, packed_recv, pair_send, pair_recv,
    half_send, half_recv, rows_send, rows_recv, back_send, back_recv, home_send, home_recv,
    twin_send, twin_recv, chip_send, chip_recv,
):
    z = lax.axis_index("pipe")
    d = lax.axis_index("dp")
    core = d % 2
    chip = d // 2
    px, py = chip // SIDE, chip % SIDE
    twin = chip * 2 + 1 - core
    z_next, z_before = (z + 1) % SECTIONS, (z + SECTIONS - 1) % SECTIONS

    def remote(src, dst, send, recv, to_z, to_d):
        return pltpu.make_async_remote_copy(
            src_ref=src, dst_ref=dst, send_sem=send, recv_sem=recv,
            device_id={"pipe": to_z, "dp": to_d}, device_id_type=MESH,
        )

    def await_recv(ref, sem):
        remote(ref, ref, sem, sem, z, twin).wait_recv()

    def await_send(ref, sem):
        remote(ref, ref, sem, sem, z, twin).wait_send()

    def loop(low, high, run):
        lax.fori_loop(low, high, lambda i, c: (run(i), c)[1], 0)

    owned = []
    for v in range(2):
        own = weight.at[v * SECTIONS + z]
        owned.append(pltpu.make_async_copy(
            key_ref.at[v], own.at[:, :, :, :, pl.ds(0, HEAD)], own_sem.at[v, 0]))
        owned.append(pltpu.make_async_copy(
            value_ref.at[v], own.at[:, :, :, :, pl.ds(HEAD, HEAD)], own_sem.at[v, 1]))
    for copy in owned:
        copy.start()
    upstream_rows = pl.ds(pl.multiple_of(z // 2 * 2 * ROWS, 2 * ROWS), 2 * ROWS)
    last_copy = pltpu.make_async_copy(cotangent_ref.at[upstream_rows, :], last, last_sem)
    last_copy.start()
    for v in range(2):
        gains[z, v] = jnp.concatenate(
            [gain_ref[v:v + 1, HEAD * h:HEAD * (h + 1)] for h in range(HEADS)], axis=0)

    row = lax.broadcasted_iota(jnp.int32, (2 * TILE, 2 * TILE), 0)
    col = lax.broadcasted_iota(jnp.int32, (2 * TILE, 2 * TILE), 1)
    kind_row = (col // TILE) * (ROWS // 2) + col % (ROWS // 2)
    micro = lax.broadcasted_iota(jnp.int32, (SECTIONS, 2 * TILE), 0)
    lane = lax.broadcasted_iota(jnp.int32, (SECTIONS, 2 * TILE), 1) % TILE
    spread_out = jnp.where(micro == lane // ROWS, 1.0, 0.0).astype(BF16)
    lane_route = dot(route_ref[...].astype(F32).astype(BF16), spread_out, 1, 0)
    leading = lane[0:1] // (ROWS // 2) % 2 == 0
    lane_route = jnp.where(leading, lane_route[0:1], lane_route[1:2])
    chosen = (lane_route == (row // ROWS).astype(F32)) & (row % ROWS == kind_row)
    sort = jnp.where(chosen, 1.0, 0.0).astype(BF16)
    sorting[...] = sort[:, :TILE]
    row = lax.broadcasted_iota(jnp.int32, (TILE, SECTIONS), 0)
    col = lax.broadcasted_iota(jnp.int32, (TILE, SECTIONS), 1)
    spread_out = jnp.where(row // ROWS == col, 1.0, 0.0).astype(BF16)
    row_lengths = dot(spread_out, lengths_ref[...].astype(F32).astype(BF16), 1, 1)
    row = lax.broadcasted_iota(jnp.int32, (TILE, HEAD), 0)
    lane = lax.broadcasted_iota(jnp.int32, (TILE, HEAD), 1)
    at = (row % ROWS).astype(F32)
    ends = [jnp.broadcast_to(row_lengths[:, 0:1], (TILE, HEAD))]
    for k in range(1, row_lengths.shape[1] - 1):
        ends.append(ends[-1] + row_lengths[:, k:k + 1])
    document = jnp.zeros((TILE, HEAD), F32)
    opening = jnp.zeros((TILE, HEAD), F32)
    for end in ends:
        document = document + jnp.where(at >= end, 1.0, 0.0)
        opening = jnp.where(at >= end, end, opening)
    slots = (row // (ROWS // 2)).astype(F32)
    tags = jnp.where(lane < HEAD // 4, document, jnp.where(lane < HEAD // 2, at - opening, slots))
    source = jnp.concatenate([hidden_ref[...], tags.astype(BF16)], axis=0)
    half_out[...] = dot(sort, source, 1, 0).reshape(GROUPS, ROWS, HEAD)
    half_in[d] = half_out[d]

    barrier = pltpu.get_barrier_semaphore()

    def greet_plane(k):
        pl.semaphore_signal(
            barrier, inc=1, device_id={"pipe": z, "dp": (d + k) % GROUPS}, device_id_type=MESH)

    def greet_line(k):
        pl.semaphore_signal(
            barrier, inc=1, device_id={"pipe": (z + k) % SECTIONS, "dp": d}, device_id_type=MESH)

    loop(1, GROUPS, greet_plane)
    loop(1, SECTIONS, greet_line)
    pl.semaphore_wait(barrier, GROUPS + SECTIONS - 2)

    def send_half(k):
        to = (d + k) % GROUPS
        remote(half_out.at[to], half_in.at[d], half_send.at[to], half_recv.at[d], z, to).start()

    for copy in owned:
        copy.wait()

    def row_of(layer, e):
        return weight.at[layer, :, py, core] if e == 0 else weight.at[layer, px, :, core]

    def line_step(v, s):
        on_left = (z + SECTIONS - s) % SECTIONS
        on_right = (z + s) % SECTIONS
        left_rows = row_of(v * SECTIONS + on_left, 0)
        right_rows = row_of(v * SECTIONS + on_right, 1)

        @pl.when(s >= 1)
        def _():
            await_recv(left_rows, zw_recv.at[v, on_left])

        @pl.when(s <= 7)
        def _():
            remote(left_rows, left_rows, zw_right.at[v, s], zw_recv.at[v, on_left], z_next, d).start()

        @pl.when((s >= 1) & (s <= 7))
        def _():
            await_recv(right_rows, zw_recv.at[v, on_right])

        @pl.when(s <= 6)
        def _():
            remote(right_rows, right_rows, zw_left.at[v, s], zw_recv.at[v, on_right], z_before, d).start()

    def gain_step(s):
        on_left = (z + SECTIONS - s) % SECTIONS
        on_right = (z + s) % SECTIONS

        @pl.when(s >= 1)
        def _():
            await_recv(gains.at[on_left], zg_recv.at[on_left])

        @pl.when(s <= 7)
        def _():
            line = gains.at[on_left]
            remote(line, line, zg_right.at[s], zg_recv.at[on_left], z_next, d).start()

        @pl.when((s >= 1) & (s <= 7))
        def _():
            await_recv(gains.at[on_right], zg_recv.at[on_right])

        @pl.when(s <= 6)
        def _():
            line = gains.at[on_right]
            remote(line, line, zg_left.at[s], zg_recv.at[on_right], z_before, d).start()

    line_step(0, 0)
    gain_step(0)
    loop(1, GROUPS, send_half)

    def await_half(k):
        at = (d + k) % GROUPS
        await_recv(half_in.at[at], half_recv.at[at])

    def send_rows(k):
        to = (z + k) % SECTIONS
        remote(rows_out.at[to], rows_in.at[z], rows_send.at[to], rows_recv.at[z], to, d).start()

    def place_halves():
        loop(1, GROUPS, await_half)
        arrived = half_in[...]
        slot = jnp.broadcast_to(arrived[:, 4:5, HEAD // 2:HEAD // 2 + 1], (GROUPS, ROWS, 1))
        slot = slot.reshape(2 * TILE, 1)
        arrived = arrived.reshape(2 * TILE, HEAD).astype(BF16)
        row = lax.broadcasted_iota(jnp.int32, (2 * TILE, TILE), 0) % ROWS
        col = lax.broadcasted_iota(jnp.int32, (2 * TILE, TILE), 1)
        same = slot == (col // (ROWS // 2)).astype(F32)
        place = jnp.where(same & (row == col % (ROWS // 2)), 1.0, 0.0).astype(BF16)
        place_tags = jnp.where(same & (row == col % (ROWS // 2) + ROWS // 2), 1.0, 0.0).astype(BF16)
        placing[...] = place
        rows_out[...] = dot(place, arrived, 0, 0).reshape(SECTIONS, ROWS, HEAD)
        home_out[pl.ds(0, SECTIONS)] = dot(place_tags, arrived, 0, 0).reshape(SECTIONS, ROWS, HEAD)
        rows_in[z] = rows_out[z]

        loop(1, SECTIONS, send_rows)

        tags = home_out[z]
        document = jnp.broadcast_to(tags[:, 0:1], (ROWS, TILE))
        position = jnp.broadcast_to(tags[:, HEAD // 4:HEAD // 4 + 1], (ROWS, TILE))
        lane = lax.broadcasted_iota(jnp.int32, (ROWS, TILE), 1) % ROWS
        mine = lane == lax.broadcasted_iota(jnp.int32, (ROWS, TILE), 0)
        query_document = jnp.sum(jnp.where(mine, document, 0.0), axis=0, keepdims=True)
        query_position = jnp.sum(jnp.where(mine, position, 0.0), axis=0, keepdims=True)
        allowed = (document == query_document) & (position <= query_position)
        bias[...] = jnp.where(allowed, 0.0, NEGATIVE)
        lane = lax.broadcasted_iota(jnp.int32, (ROWS, HEAD), 1)
        power = (lane % (HEAD // 2)).astype(F32) * (-2.0 / HEAD)
        angles = position * jnp.exp(power * math.log(ROPE_BASE))
        sine = jnp.sin(angles)
        turns[0] = jnp.cos(angles)
        turns[1] = jnp.where(lane < HEAD // 2, -sine, sine)

    def await_rows(k):
        at = (z + k) % SECTIONS
        await_recv(rows_in.at[at], rows_recv.at[at])

    def take_rows():
        loop(1, SECTIONS, await_rows)
        current[...] = rows_in[...].reshape(TILE, HEAD)

    def partner(j):
        return (z + jnp.where(j % 2 == 1, (j + 1) // 2, SECTIONS - j // 2)) % SECTIONS

    def send_packed(v, j):
        to = partner(j)
        remote(packed_all.at[v * SECTIONS + to], packed_in.at[v, z],
               packed_send.at[v, to], packed_recv.at[v, z], to, d).start()

    def send_pairs(v, j):
        to = partner(j)
        remote(pairs_all.at[v * SECTIONS + to], pairs_in.at[v, z],
               pair_send.at[v, to], pair_recv.at[v, z], to, d).start()

    def forward(layer):
        cosine, sine = turns[0], turns[1]
        cosine_all, sine_all = over_heads(cosine), over_heads(sine)
        x = current[...]
        saved[layer] = x
        scale = lax.rsqrt(row_mean(x * x) + EPSILON)
        saved_scale[layer] = scale
        normed = x * over_heads(scale) * gain_rows(gains[layer % SECTIONS, layer // SECTIONS])
        wide = side_by_side(normed)
        pre = dot(wide.astype(BF16), weight[layer].reshape(FEATURES, 2 * HEAD), 1, 0)
        packed = jnp.concatenate(
            [wide[:, :FEATURES // 2], wide[:, FEATURES // 2:]], axis=0).astype(BF16)
        packed_all[layer] = packed
        owner, v = layer % SECTIONS, layer // SECTIONS

        @pl.when(owner == z)
        def _():
            packed_in[v, z] = packed

        keys = turn(pre[:, :HEAD], cosine, sine).astype(BF16)
        values = pre[:, HEAD:].astype(BF16)
        queries = turn(normed, cosine_all, sine_all).astype(BF16)
        scores = dot(keys, queries, 1, 1) * HEAD ** (-0.5) + bias[...]
        raised = jnp.exp(scores - jnp.max(scores, axis=0, keepdims=True))
        weights = raised / jnp.sum(raised, axis=0, keepdims=True)
        saved_queries[layer] = queries
        saved_keys[layer, 0] = keys
        saved_keys[layer, 1] = values
        saved_weights[layer] = weights
        current[...] = x + dot(weights.astype(BF16), values, 0, 0)

    def rows_at(layer, e, at, rows):
        if e == 0:
            return weight.at[layer, :, at, core, rows, :]
        return weight.at[layer, at, :, core, rows, :]

    def device_by(e, by):
        if e == 0:
            return (px * SIDE + (py + by) % SIDE) * 2 + core
        return (((px + by) % SIDE) * SIDE + py) * 2 + core

    def around(e, by):
        return ((py if e == 0 else px) + by) % SIDE

    every, low, high = pl.ds(0, PART), pl.ds(0, PART // 2), pl.ds(PART // 2, PART // 2)

    def stage_one(layer, e):
        line = rows_at(layer, e, around(e, 0), every)
        remote(line, line, ring_send.at[layer, 0], ring_recv.at[layer, 0], z, device_by(e, 1)).start()
        remote(line, line, ring_send.at[layer, 0], ring_recv.at[layer, 1], z, device_by(e, 3)).start()

    def stage_two(layer, e):
        left, right = around(e, 3), around(e, 1)
        await_recv(rows_at(layer, e, left, every), ring_recv.at[layer, 0])
        part = rows_at(layer, e, left, low)
        remote(part, part, ring_send.at[layer, 1], ring_recv.at[layer, 2], z, device_by(e, 1)).start()
        await_recv(rows_at(layer, e, right, every), ring_recv.at[layer, 1])
        part = rows_at(layer, e, right, high)
        remote(part, part, ring_send.at[layer, 1], ring_recv.at[layer, 3], z, device_by(e, 3)).start()

    def stage_three(layer, e):
        far = around(e, 2)
        await_recv(rows_at(layer, e, far, low), ring_recv.at[layer, 2])
        await_recv(rows_at(layer, e, far, high), ring_recv.at[layer, 3])
        half = weight.at[layer, :, :, core]
        remote(half, half, ring_send.at[layer, 2], ring_recv.at[layer, 4], z, twin).start()

    def stage_four(layer, e):
        await_recv(weight.at[layer, :, :, 1 - core], ring_recv.at[layer, 4])

    def turn_of(t):
        @pl.when((t >= 1) & (t <= 8))
        def _():
            line_step(0, t)
            gain_step(t)

        @pl.when((t <= 7) & (t % 2 == 1))
        def _():
            line_step(1, t // 2)

        @pl.when((t >= 8) & (t <= 12))
        def _():
            line_step(1, t - 4)

        for late, stage in ((0, stage_one), (1, stage_two), (2, stage_three), (3, stage_four)):
            v = jnp.where(t - late <= 8, 0, 1)
            s = t - late - 8 * v

            @pl.when((s >= 1) & (s <= 8))
            def _():
                stage(v * SECTIONS + (z + SECTIONS - s) % SECTIONS, 0)

            @pl.when((s >= 1) & (s <= 7))
            def _():
                stage(v * SECTIONS + (z + s) % SECTIONS, 1)

        @pl.when(t == 3)
        def _():
            place_halves()

        @pl.when(t == 11)
        def _():
            take_rows()

        @pl.when((t >= 11) & (t <= 14))
        def _():
            loop(4 * (t - 11), 4 * (t - 11) + 4, forward)

        @pl.when(t >= 15)
        def _():
            for k in range(1, 4):
                send_packed(0, 3 * (t - 15) + k)

    loop(1, 20, turn_of)

    loop(SECTIONS, LAYERS, forward)

    last_copy.wait()
    both = last[...].astype(F32)
    current[...] = stacked(jnp.where(z % 2 == 0, both[:ROWS], both[ROWS:]))

    def backward(step):
        layer = LAYERS - 1 - step
        cosine, sine = turns[0], turns[1]
        cosine_all, sine_all = over_heads(cosine), over_heads(sine)
        upstream = current[...]
        rounded = upstream.astype(BF16)
        keys = saved_keys[layer, 0]
        values = saved_keys[layer, 1]
        weights = saved_weights[layer]
        d_weights = dot(values, rounded, 1, 1).astype(BF16).astype(F32)
        d_values = dot(weights.astype(BF16), rounded, 1, 0).astype(BF16).astype(F32)
        inner = jnp.sum(d_weights * weights, axis=0, keepdims=True)
        d_scores = (weights * (d_weights - inner) * HEAD ** (-0.5)).astype(BF16)
        d_queries = dot(d_scores, keys, 0, 0).astype(BF16).astype(F32)
        d_keys = dot(d_scores, saved_queries[layer], 1, 0).astype(BF16).astype(F32)
        d_key_pre = unturn(d_keys, cosine, sine)
        pair = jnp.concatenate([d_key_pre, d_values], axis=1).astype(BF16)
        pair_rows = jnp.concatenate([d_key_pre, d_values], axis=0).astype(BF16)
        pairs_all[layer] = pair_rows
        owner, v = layer % SECTIONS, layer // SECTIONS

        @pl.when(owner == z)
        def _():
            pairs_in[v, z] = pair_rows

        d_packed = stacked(
            dot(pair, weight[layer].reshape(FEATURES, 2 * HEAD), 1, 1))
        d_normed = unturn(d_queries, cosine_all, sine_all) + d_packed
        x = saved[layer]
        scale = saved_scale[layer]
        scaled = d_normed * gain_rows(gains[layer % SECTIONS, layer // SECTIONS])
        pull = row_mean(scaled * x) * scale * scale * scale
        current[...] = upstream + scaled * over_heads(scale) - x * over_heads(pull)

    def terms_of(v):
        def await_rows_of(k):
            at = (z + k) % SECTIONS
            await_recv(packed_in.at[v, at], packed_recv.at[v, at])
            await_recv(pairs_in.at[v, at], pair_recv.at[v, at])

        loop(1, SECTIONS, await_rows_of)
        pair = pairs_in[v].astype(F32)
        pair = jnp.concatenate([pair[:, :ROWS], pair[:, ROWS:]], axis=2)
        nothing = jnp.zeros_like(pair)
        upper = jnp.concatenate([pair, nothing], axis=1).reshape(2 * TILE, 2 * HEAD)
        lower = jnp.concatenate([nothing, pair], axis=1).reshape(2 * TILE, 2 * HEAD)
        both = jnp.concatenate([upper, lower], axis=1).astype(BF16)
        product = dot(packed_in[v].reshape(2 * TILE, FEATURES // 2), both, 0, 0).astype(BF16)
        for g in range(GROUPS):
            rows = product[PART * (g % 16):PART * (g % 16 + 1)]
            terms[v, g // 2, g % 2] = rows[:, 2 * HEAD * (g // 16):2 * HEAD * (g // 16 + 1)]
        remote(terms.at[v, :, 1 - core], twin_in.at[v],
               twin_send.at[v], twin_recv.at[v], z, twin).start()

    def send_chips(v):
        await_recv(twin_in.at[v], twin_recv.at[v])
        chip_terms[v] = (terms[v, :, core].astype(F32) + twin_in[v].astype(F32)).astype(BF16)

        def send_chip(k):
            to = (chip + k) % (GROUPS // 2)
            remote(chip_terms.at[v, to], chip_in.at[v, chip],
                   chip_send.at[v, to], chip_recv.at[v, chip], z, 2 * to + core).start()

        loop(1, GROUPS // 2, send_chip)
        chip_in[v, chip] = chip_terms[v, chip]

    def backward_step(j):
        backward(j)

        @pl.when((j >= 1) & (j < SECTIONS))
        def _():
            send_packed(1, j)

        @pl.when((j >= SECTIONS) & (j < SECTIONS + 8))
        def _():
            send_pairs(1, 2 * (j - SECTIONS) + 1)

        @pl.when((j >= SECTIONS) & (j < SECTIONS + 7))
        def _():
            send_pairs(1, 2 * (j - SECTIONS) + 2)

        @pl.when(j == 27)
        def _():
            terms_of(1)

        @pl.when(j == 30)
        def _():
            send_chips(1)

    loop(0, LAYERS, backward_step)
    loop(1, SECTIONS, lambda j: send_pairs(0, j))

    back_out[...] = current[...].astype(BF16).astype(F32).reshape(SECTIONS, ROWS, HEAD)
    back_in[z] = back_out[z]

    def send_back(k):
        to = (z + k) % SECTIONS
        remote(back_out.at[to], back_in.at[z], back_send.at[to], back_recv.at[z], to, d).start()

    loop(1, SECTIONS, send_back)
    terms_of(0)

    def await_back(k):
        at = (z + k) % SECTIONS
        await_recv(back_in.at[at], back_recv.at[at])

    loop(1, SECTIONS, await_back)
    mine = back_in[...].reshape(TILE, HEAD).astype(BF16)
    home_out[...] = dot(placing[...], mine, 1, 0).reshape(GROUPS, ROWS, HEAD)
    home_in[d] = home_out[d]

    def send_home(k):
        to = (d + k) % GROUPS
        remote(home_out.at[to], home_in.at[d], home_send.at[to], home_recv.at[d], z, to).start()

    loop(1, GROUPS, send_home)
    send_chips(0)

    def await_home(k):
        at = (d + k) % GROUPS
        await_recv(home_in.at[at], home_recv.at[at])

    loop(1, GROUPS, await_home)
    arrived = home_in[...].reshape(2 * TILE, HEAD).astype(BF16)
    grad_ref[...] = dot(sorting[...], arrived, 0, 0).astype(BF16)

    def sent_layer(layer):
        @pl.when(layer % SECTIONS != z)
        def _():
            await_send(weight.at[layer, pl.ds(0, 2), :, 0], ring_send.at[layer, 0])
            await_send(weight.at[layer, 0, :, 0], ring_send.at[layer, 1])
            await_send(weight.at[layer, :, :, 0], ring_send.at[layer, 2])
            await_send(packed_all.at[layer], packed_send.at[layer // SECTIONS, layer % SECTIONS])
            await_send(pairs_all.at[layer], pair_send.at[layer // SECTIONS, layer % SECTIONS])

    loop(0, LAYERS, sent_layer)

    def sent_line(s):
        await_send(gains.at[0], zg_right.at[s])
        for v in range(2):
            await_send(row_of(0, 0), zw_right.at[v, s])

        @pl.when(s <= 6)
        def _():
            await_send(gains.at[0], zg_left.at[s])
            for v in range(2):
                await_send(row_of(0, 1), zw_left.at[v, s])

    loop(0, 8, sent_line)

    def sent_plane(k):
        to = (d + k) % GROUPS
        await_send(half_out.at[to], half_send.at[to])
        await_send(home_out.at[to], home_send.at[to])

    def sent_sections(k):
        to = (z + k) % SECTIONS
        await_send(rows_out.at[to], rows_send.at[to])
        await_send(back_out.at[to], back_send.at[to])

    loop(1, GROUPS, sent_plane)
    loop(1, SECTIONS, sent_sections)

    for v in range(2):
        await_send(twin_in.at[v], twin_send.at[v])

        def await_chip(k):
            at = (chip + k) % (GROUPS // 2)
            await_recv(chip_in.at[v, at], chip_recv.at[v, at])
            await_send(chip_terms.at[v, at], chip_send.at[v, at])

        loop(1, GROUPS // 2, await_chip)
        total = jnp.zeros((PART, 2 * HEAD), F32)
        for k in range(GROUPS // 2):
            total = total + chip_in[v, k].astype(F32)
        key_out_ref[v] = total[:, :HEAD]
        value_out_ref[v] = total[:, HEAD:]


def run_whole(hidden, lengths, route, gain, key_weight, value_weight, cotangent):
    whole = pl.BlockSpec(memory_space=pltpu.VMEM)
    remote = pl.BlockSpec(memory_space=pl.ANY)
    dma = pltpu.SemaphoreType.DMA
    small = pltpu.VMEM((SECTIONS, ROWS, HEAD), F32)
    large = pltpu.VMEM((GROUPS, ROWS, HEAD), F32)
    chips = GROUPS // 2
    return pl.pallas_call(
        whole_kernel,
        out_shape=(
            jax.ShapeDtypeStruct((TILE, HEAD), BF16),
            jax.ShapeDtypeStruct((2, PART, HEAD), F32),
            jax.ShapeDtypeStruct((2, PART, HEAD), F32),
        ),
        in_specs=[whole] * 4 + [remote] * 3,
        out_specs=(whole, whole, whole),
        scratch_shapes=[
            pltpu.VMEM((LAYERS, SIDE, SIDE, 2, PART, 2 * HEAD), BF16),
            pltpu.VMEM((SECTIONS, 2, HEADS, HEAD), F32),
            pltpu.VMEM((TILE, HEAD), F32),
            pltpu.VMEM((LAYERS, TILE, HEAD), F32),
            pltpu.VMEM((LAYERS, TILE, HEAD), BF16),
            pltpu.VMEM((LAYERS, 2, ROWS, HEAD), BF16),
            pltpu.VMEM((LAYERS, ROWS, TILE), F32),
            pltpu.VMEM((LAYERS, ROWS, 1), F32),
            pltpu.VMEM((ROWS, TILE), F32),
            pltpu.VMEM((2, ROWS, HEAD), F32),
            pltpu.VMEM((LAYERS, 2 * ROWS, FEATURES // 2), BF16),
            pltpu.VMEM((2, SECTIONS, 2 * ROWS, FEATURES // 2), BF16),
            pltpu.VMEM((LAYERS, 2 * ROWS, HEAD), BF16),
            pltpu.VMEM((2, SECTIONS, 2 * ROWS, HEAD), BF16),
            pltpu.VMEM((2, chips, 2, PART, 2 * HEAD), BF16),
            pltpu.VMEM((2, chips, PART, 2 * HEAD), BF16),
            pltpu.VMEM((2, chips, PART, 2 * HEAD), BF16),
            pltpu.VMEM((2, chips, PART, 2 * HEAD), BF16),
            pltpu.VMEM((2 * TILE, TILE), BF16),
            pltpu.VMEM((2 * TILE, TILE), BF16),
            large, large, small, small, small, small, large, large,
            pltpu.VMEM((2 * ROWS, FEATURES), BF16),
            dma(()), dma((2, 2)),
            dma((2, SECTIONS)), dma((2, 8)), dma((2, 8)),
            dma((SECTIONS,)), dma((8,)), dma((8,)),
            dma((LAYERS, 3)), dma((LAYERS, 5)),
            dma((2, SECTIONS)), dma((2, SECTIONS)), dma((2, SECTIONS)), dma((2, SECTIONS)),
            dma((GROUPS,)), dma((GROUPS,)), dma((SECTIONS,)), dma((SECTIONS,)),
            dma((SECTIONS,)), dma((SECTIONS,)), dma((GROUPS,)), dma((GROUPS,)),
            dma((2,)), dma((2,)), dma((2, chips)), dma((2, chips)),
        ],
        compiler_params=pltpu.CompilerParams(
            collective_id=0, has_side_effects=True, vmem_limit_bytes=56 * 2**20),
    )(hidden, lengths, route, gain, key_weight, value_weight, cotangent)


def body(hidden, lengths, route, gain, key_weight, value_weight, cotangent):
    shares = (2, SIDE, SIDE, 2, PART, HEAD)
    return run_whole(
        hidden, lengths.T, route.T, gain,
        key_weight.reshape(shares), value_weight.reshape(shares), cotangent)


def solution(mesh):
    placed = (
        P("dp", "pipe"),
        P("dp", None),
        P("dp", None),
        P("pipe", None),
        P("pipe", None, None),
        P("pipe", None, None),
        P("dp", None),
    )
    return jax.shard_map(
        body,
        mesh=mesh,
        in_specs=placed,
        out_specs=(P("dp", "pipe"), P("pipe", "dp", None), P("pipe", "dp", None)),
        check_vma=False,
    )
```

time: 249 us -> 196 us (0.79); the launches traced: 244 us -> 196 us
  Pallas kernels: 234 us -> 192 us
  local copies, waits for them, and re-layouts: 6.61 us -> 2.9 us
  other arithmetic: 2.95 us -> 0 us
    pallas_call x1, Pallas kernels: 234 us -> 192 us  [run_whole(): pl.pallas_call(whole_kernel, out_shape=(jax.ShapeDtypeStruct((TILE, HEAD)...]
    unnamed x17 -> x7, local copies, waits for them, and re-layouts: 5.38 us -> 2.9 us
where the time goes in v3:
time: 196 us
  Pallas kernels  192 us (98%)
  local copies, waits for them, and re-layouts  2.9 us (1%)
    pallas_call x1, Pallas kernels, run_whole(): pl.pallas_call(whole_kernel, out_shape=(jax.ShapeDtypeStruct((TILE, HEAD)...  192 us

profile of v3, /device:TPU:1, one launch (start us, length us, event | category | flops | bytes accessed | tf_op | source)
XLA Modules:
  0.0 195.7 jit_solution(15564571387388708772)
XLA Ops:
  0.6 192.2 %shard_map.94 = (bf16[128,128]{1,0:T(8,128)(2,1)}, f32[2,64,128]{2,1,0:T(8,128)}, f32[2,64,128]{2,1,0:T(8,128)}) custom-call(bf16[128,128]{1,0:T(8,128)(2,1)} %hidden_ref.1, s32[4,16]{1,0:T(4,128)} %bitcast.6, s32[2,16]{1,0:T(2,128)} %bitcast.7, f32[2,2048]{1,0:T(2,128)} %gain_ref.1, bf16[2,4,4,2,64,128]{5,4,3,2,1,0:T(8,128)(2,1)} %bitcast.4, ...), custom_call_target="tpu_custom_call" | custom-call | tf_op jit(solution)/shard_map/pallas_call | solution.py:594
  192.8 0.0 copy-start.1
  192.8 1.4 copy.13
  194.2 0.0 copy-done.1
  194.2 0.0 copy-start
  194.2 0.6 copy.14
  194.8 0.2 copy-done
  195.1 0.6 copy.15
Async XLA Ops:
  192.8 1.4 copy-start.1
  194.2 0.9 copy-start

commit v4 on v3

--- a/solution.py
+++ b/solution.py
@@ -85,6 +85,22 @@
     twin = chip * 2 + 1 - core
     z_next, z_before = (z + 1) % SECTIONS, (z + SECTIONS - 1) % SECTIONS
 
+    def loop(low, high, run):
+        lax.fori_loop(low, high, lambda i, c: (run(i), c)[1], 0)
+
+    barrier = pltpu.get_barrier_semaphore()
+
+    def greet_plane(k):
+        pl.semaphore_signal(
+            barrier, inc=1, device_id={"pipe": z, "dp": (d + k) % GROUPS}, device_id_type=MESH)
+
+    def greet_line(k):
+        pl.semaphore_signal(
+            barrier, inc=1, device_id={"pipe": (z + k) % SECTIONS, "dp": d}, device_id_type=MESH)
+
+    loop(1, GROUPS, greet_plane)
+    loop(1, SECTIONS, greet_line)
+
     def remote(src, dst, send, recv, to_z, to_d):
         return pltpu.make_async_remote_copy(
             src_ref=src, dst_ref=dst, send_sem=send, recv_sem=recv,
@@ -96,9 +112,6 @@
 
     def await_send(ref, sem):
         remote(ref, ref, sem, sem, z, twin).wait_send()
-
-    def loop(low, high, run):
-        lax.fori_loop(low, high, lambda i, c: (run(i), c)[1], 0)
 
     owned = []
     for v in range(2):
@@ -149,23 +162,11 @@
     half_out[...] = dot(sort, source, 1, 0).reshape(GROUPS, ROWS, HEAD)
     half_in[d] = half_out[d]
 
-    barrier = pltpu.get_barrier_semaphore()
-
-    def greet_plane(k):
-        pl.semaphore_signal(
-            barrier, inc=1, device_id={"pipe": z, "dp": (d + k) % GROUPS}, device_id_type=MESH)
-
-    def greet_line(k):
-        pl.semaphore_signal(
-            barrier, inc=1, device_id={"pipe": (z + k) % SECTIONS, "dp": d}, device_id_type=MESH)
-
-    loop(1, GROUPS, greet_plane)
-    loop(1, SECTIONS, greet_line)
     pl.semaphore_wait(barrier, GROUPS + SECTIONS - 2)
 
     def send_half(k):
         to = (d + k) % GROUPS
-        remote(half_out.at[to], half_in.at[d], half_send.at[to], half_recv.at[d], z, to).start()
+        remote(half_out.at[to], half_in.at[d], half_send, half_recv, z, to).start()
 
     for copy in owned:
         copy.wait()
@@ -176,24 +177,27 @@
     def line_step(v, s):
         on_left = (z + SECTIONS - s) % SECTIONS
         on_right = (z + s) % SECTIONS
-        left_rows = row_of(v * SECTIONS + on_left, 0)
-        right_rows = row_of(v * SECTIONS + on_right, 1)
-
-        @pl.when(s >= 1)
-        def _():
-            await_recv(left_rows, zw_recv.at[v, on_left])
-
-        @pl.when(s <= 7)
-        def _():
-            remote(left_rows, left_rows, zw_right.at[v, s], zw_recv.at[v, on_left], z_next, d).start()
-
-        @pl.when((s >= 1) & (s <= 7))
-        def _():
-            await_recv(right_rows, zw_recv.at[v, on_right])
-
-        @pl.when(s <= 6)
-        def _():
-            remote(right_rows, right_rows, zw_left.at[v, s], zw_recv.at[v, on_right], z_before, d).start()
+        for q in range(SIDE):
+            left = weight.at[v * SECTIONS + on_left, q, py, core]
+            right = weight.at[v * SECTIONS + on_right, px, q, core]
+            left_sem = zw_recv.at[v, on_left, q]
+            right_sem = zw_recv.at[v, on_right, q]
+
+            @pl.when(s >= 1)
+            def _():
+                await_recv(left, left_sem)
+
+            @pl.when(s <= 7)
+            def _():
+                remote(left, left, zw_right.at[v], left_sem, z_next, d).start()
+
+            @pl.when((s >= 1) & (s <= 7))
+            def _():
+                await_recv(right, right_sem)
+
+            @pl.when(s <= 6)
+            def _():
+                remote(right, right, zw_left.at[v], right_sem, z_before, d).start()
 
     def gain_step(s):
         on_left = (z + SECTIONS - s) % SECTIONS
@@ -206,7 +210,7 @@
         @pl.when(s <= 7)
         def _():
             line = gains.at[on_left]
-            remote(line, line, zg_right.at[s], zg_recv.at[on_left], z_next, d).start()
+            remote(line, line, zg_right, zg_recv.at[on_left], z_next, d).start()
 
         @pl.when((s >= 1) & (s <= 7))
         def _():
@@ -215,22 +219,18 @@
         @pl.when(s <= 6)
         def _():
             line = gains.at[on_right]
-            remote(line, line, zg_left.at[s], zg_recv.at[on_right], z_before, d).start()
+            remote(line, line, zg_left, zg_recv.at[on_right], z_before, d).start()
 
     line_step(0, 0)
     gain_step(0)
     loop(1, GROUPS, send_half)
 
-    def await_half(k):
-        at = (d + k) % GROUPS
-        await_recv(half_in.at[at], half_recv.at[at])
-
     def send_rows(k):
         to = (z + k) % SECTIONS
-        remote(rows_out.at[to], rows_in.at[z], rows_send.at[to], rows_recv.at[z], to, d).start()
+        remote(rows_out.at[to], rows_in.at[z], rows_send, rows_recv, to, d).start()
 
     def place_halves():
-        loop(1, GROUPS, await_half)
+        await_recv(half_in.at[pl.ds(0, GROUPS - 1)], half_recv)
         arrived = half_in[...]
         slot = jnp.broadcast_to(arrived[:, 4:5, HEAD // 2:HEAD // 2 + 1], (GROUPS, ROWS, 1))
         slot = slot.reshape(2 * TILE, 1)
@@ -263,12 +263,8 @@
         turns[0] = jnp.cos(angles)
         turns[1] = jnp.where(lane < HEAD // 2, -sine, sine)
 
-    def await_rows(k):
-        at = (z + k) % SECTIONS
-        await_recv(rows_in.at[at], rows_recv.at[at])
-
     def take_rows():
-        loop(1, SECTIONS, await_rows)
+        await_recv(rows_in.at[pl.ds(0, SECTIONS - 1)], rows_recv)
         current[...] = rows_in[...].reshape(TILE, HEAD)
 
     def partner(j):
@@ -277,35 +273,28 @@
     def send_packed(v, j):
         to = partner(j)
         remote(packed_all.at[v * SECTIONS + to], packed_in.at[v, z],
-               packed_send.at[v, to], packed_recv.at[v, z], to, d).start()
+               packed_send.at[v], packed_recv.at[v], to, d).start()
 
     def send_pairs(v, j):
         to = partner(j)
         remote(pairs_all.at[v * SECTIONS + to], pairs_in.at[v, z],
-               pair_send.at[v, to], pair_recv.at[v, z], to, d).start()
+               pair_send.at[v], pair_recv.at[v], to, d).start()
 
     def forward(layer):
         cosine, sine = turns[0], turns[1]
         cosine_all, sine_all = over_heads(cosine), over_heads(sine)
         x = current[...]
         saved[layer] = x
+        gained = x * gain_rows(gains[layer % SECTIONS, layer // SECTIONS])
+        pre = dot(side_by_side(gained).astype(BF16),
+                  weight[layer].reshape(FEATURES, 2 * HEAD), 1, 0)
         scale = lax.rsqrt(row_mean(x * x) + EPSILON)
         saved_scale[layer] = scale
-        normed = x * over_heads(scale) * gain_rows(gains[layer % SECTIONS, layer // SECTIONS])
-        wide = side_by_side(normed)
-        pre = dot(wide.astype(BF16), weight[layer].reshape(FEATURES, 2 * HEAD), 1, 0)
-        packed = jnp.concatenate(
-            [wide[:, :FEATURES // 2], wide[:, FEATURES // 2:]], axis=0).astype(BF16)
-        packed_all[layer] = packed
-        owner, v = layer % SECTIONS, layer // SECTIONS
-
-        @pl.when(owner == z)
-        def _():
-            packed_in[v, z] = packed
-
+        pre = pre * scale
+        normed = gained * over_heads(scale)
+        queries = turn(normed, cosine_all, sine_all).astype(BF16)
         keys = turn(pre[:, :HEAD], cosine, sine).astype(BF16)
         values = pre[:, HEAD:].astype(BF16)
-        queries = turn(normed, cosine_all, sine_all).astype(BF16)
         scores = dot(keys, queries, 1, 1) * HEAD ** (-0.5) + bias[...]
         raised = jnp.exp(scores - jnp.max(scores, axis=0, keepdims=True))
         weights = raised / jnp.sum(raised, axis=0, keepdims=True)
@@ -313,6 +302,9 @@
         saved_keys[layer, 0] = keys
         saved_keys[layer, 1] = values
         saved_weights[layer] = weights
+        wide = side_by_side(normed)
+        packed_all[layer] = jnp.concatenate(
+            [wide[:, :FEATURES // 2], wide[:, FEATURES // 2:]], axis=0).astype(BF16)
         current[...] = x + dot(weights.astype(BF16), values, 0, 0)
 
     def rows_at(layer, e, at, rows):
@@ -332,24 +324,24 @@
 
     def stage_one(layer, e):
         line = rows_at(layer, e, around(e, 0), every)
-        remote(line, line, ring_send.at[layer, 0], ring_recv.at[layer, 0], z, device_by(e, 1)).start()
-        remote(line, line, ring_send.at[layer, 0], ring_recv.at[layer, 1], z, device_by(e, 3)).start()
+        remote(line, line, ring_send.at[layer // SECTIONS, 0], ring_recv.at[layer, 0], z, device_by(e, 1)).start()
+        remote(line, line, ring_send.at[layer // SECTIONS, 0], ring_recv.at[layer, 1], z, device_by(e, 3)).start()
 
     def stage_two(layer, e):
         left, right = around(e, 3), around(e, 1)
         await_recv(rows_at(layer, e, left, every), ring_recv.at[layer, 0])
         part = rows_at(layer, e, left, low)
-        remote(part, part, ring_send.at[layer, 1], ring_recv.at[layer, 2], z, device_by(e, 1)).start()
+        remote(part, part, ring_send.at[layer // SECTIONS, 1], ring_recv.at[layer, 2], z, device_by(e, 1)).start()
         await_recv(rows_at(layer, e, right, every), ring_recv.at[layer, 1])
         part = rows_at(layer, e, right, high)
-        remote(part, part, ring_send.at[layer, 1], ring_recv.at[layer, 3], z, device_by(e, 3)).start()
+        remote(part, part, ring_send.at[layer // SECTIONS, 1], ring_recv.at[layer, 3], z, device_by(e, 3)).start()
 
     def stage_three(layer, e):
         far = around(e, 2)
         await_recv(rows_at(layer, e, far, low), ring_recv.at[layer, 2])
         await_recv(rows_at(layer, e, far, high), ring_recv.at[layer, 3])
         half = weight.at[layer, :, :, core]
-        remote(half, half, ring_send.at[layer, 2], ring_recv.at[layer, 4], z, twin).start()
+        remote(half, half, ring_send.at[layer // SECTIONS, 2], ring_recv.at[layer, 4], z, twin).start()
 
     def stage_four(layer, e):
         await_recv(weight.at[layer, :, :, 1 - core], ring_recv.at[layer, 4])
@@ -392,10 +384,9 @@
         def _():
             loop(4 * (t - 11), 4 * (t - 11) + 4, forward)
 
-        @pl.when(t >= 15)
-        def _():
-            for k in range(1, 4):
-                send_packed(0, 3 * (t - 15) + k)
+        @pl.when(t == 14)
+        def _():
+            loop(1, SECTIONS, lambda j: send_packed(0, j))
 
     loop(1, 20, turn_of)
 
@@ -413,39 +404,33 @@
         rounded = upstream.astype(BF16)
         keys = saved_keys[layer, 0]
         values = saved_keys[layer, 1]
+        queries = saved_queries[layer]
         weights = saved_weights[layer]
-        d_weights = dot(values, rounded, 1, 1).astype(BF16).astype(F32)
-        d_values = dot(weights.astype(BF16), rounded, 1, 0).astype(BF16).astype(F32)
+        d_weights = dot(values, rounded, 1, 1)
+        d_values = dot(weights.astype(BF16), rounded, 1, 0)
         inner = jnp.sum(d_weights * weights, axis=0, keepdims=True)
-        d_scores = (weights * (d_weights - inner) * HEAD ** (-0.5)).astype(BF16)
-        d_queries = dot(d_scores, keys, 0, 0).astype(BF16).astype(F32)
-        d_keys = dot(d_scores, saved_queries[layer], 1, 0).astype(BF16).astype(F32)
+        d_scores = ((weights * HEAD ** (-0.5)) * (d_weights - inner)).astype(BF16)
+        d_keys = dot(d_scores, queries, 1, 0)
         d_key_pre = unturn(d_keys, cosine, sine)
         pair = jnp.concatenate([d_key_pre, d_values], axis=1).astype(BF16)
-        pair_rows = jnp.concatenate([d_key_pre, d_values], axis=0).astype(BF16)
-        pairs_all[layer] = pair_rows
-        owner, v = layer % SECTIONS, layer // SECTIONS
-
-        @pl.when(owner == z)
-        def _():
-            pairs_in[v, z] = pair_rows
-
-        d_packed = stacked(
-            dot(pair, weight[layer].reshape(FEATURES, 2 * HEAD), 1, 1))
-        d_normed = unturn(d_queries, cosine_all, sine_all) + d_packed
-        x = saved[layer]
+        d_packed = stacked(dot(pair, weight[layer].reshape(FEATURES, 2 * HEAD), 1, 1))
+        pairs_all[layer] = jnp.concatenate([d_key_pre, d_values], axis=0).astype(BF16)
+        d_queries = dot(d_scores, keys, 0, 0)
+        inside = jnp.sum((d_queries * queries.astype(F32)).reshape(HEADS, ROWS, HEAD), axis=0)
+        inside = inside + d_keys * keys.astype(F32) + d_values * values.astype(F32)
         scale = saved_scale[layer]
-        scaled = d_normed * gain_rows(gains[layer % SECTIONS, layer // SECTIONS])
-        pull = row_mean(scaled * x) * scale * scale * scale
-        current[...] = upstream + scaled * over_heads(scale) - x * over_heads(pull)
+        pull = jnp.sum(inside, axis=-1, keepdims=True) * (scale * scale * (1.0 / FEATURES))
+        by = gain_rows(gains[layer % SECTIONS, layer // SECTIONS]) * over_heads(scale)
+        known = upstream - saved[layer] * over_heads(pull)
+        known = known + unturn(d_queries, cosine_all, sine_all) * by
+        current[...] = known + d_packed * by
 
     def terms_of(v):
-        def await_rows_of(k):
-            at = (z + k) % SECTIONS
-            await_recv(packed_in.at[v, at], packed_recv.at[v, at])
-            await_recv(pairs_in.at[v, at], pair_recv.at[v, at])
-
-        loop(1, SECTIONS, await_rows_of)
+        others = pl.ds(0, SECTIONS - 1)
+        await_recv(packed_in.at[v, others], packed_recv.at[v])
+        await_recv(pairs_in.at[v, others], pair_recv.at[v])
+        packed_in[v, z] = packed_all[v * SECTIONS + z]
+        pairs_in[v, z] = pairs_all[v * SECTIONS + z]
         pair = pairs_in[v].astype(F32)
         pair = jnp.concatenate([pair[:, :ROWS], pair[:, ROWS:]], axis=2)
         nothing = jnp.zeros_like(pair)
@@ -466,7 +451,7 @@
         def send_chip(k):
             to = (chip + k) % (GROUPS // 2)
             remote(chip_terms.at[v, to], chip_in.at[v, chip],
-                   chip_send.at[v, to], chip_recv.at[v, chip], z, 2 * to + core).start()
+                   chip_send.at[v], chip_recv.at[v], z, 2 * to + core).start()
 
         loop(1, GROUPS // 2, send_chip)
         chip_in[v, chip] = chip_terms[v, chip]
@@ -474,9 +459,14 @@
     def backward_step(j):
         backward(j)
 
-        @pl.when((j >= 1) & (j < SECTIONS))
-        def _():
-            send_packed(1, j)
+        @pl.when((j >= 1) & (j < 8))
+        def _():
+            send_packed(1, 2 * j - 1)
+            send_packed(1, 2 * j)
+
+        @pl.when(j == 8)
+        def _():
+            send_packed(1, SECTIONS - 1)
 
         @pl.when((j >= SECTIONS) & (j < SECTIONS + 8))
         def _():
@@ -502,81 +492,47 @@
 
     def send_back(k):
         to = (z + k) % SECTIONS
-        remote(back_out.at[to], back_in.at[z], back_send.at[to], back_recv.at[z], to, d).start()
+        remote(back_out.at[to], back_in.at[z], back_send, back_recv, to, d).start()
 
     loop(1, SECTIONS, send_back)
     terms_of(0)
 
-    def await_back(k):
-        at = (z + k) % SECTIONS
-        await_recv(back_in.at[at], back_recv.at[at])
-
-    loop(1, SECTIONS, await_back)
+    await_recv(back_in.at[pl.ds(0, SECTIONS - 1)], back_recv)
     mine = back_in[...].reshape(TILE, HEAD).astype(BF16)
     home_out[...] = dot(placing[...], mine, 1, 0).reshape(GROUPS, ROWS, HEAD)
     home_in[d] = home_out[d]
 
     def send_home(k):
         to = (d + k) % GROUPS
-        remote(home_out.at[to], home_in.at[d], home_send.at[to], home_recv.at[d], z, to).start()
+        remote(home_out.at[to], home_in.at[d], home_send, home_recv, z, to).start()
 
     loop(1, GROUPS, send_home)
     send_chips(0)
 
-    def await_home(k):
-        at = (d + k) % GROUPS
-        await_recv(home_in.at[at], home_recv.at[at])
-
-    loop(1, GROUPS, await_home)
+    await_recv(home_in.at[pl.ds(0, GROUPS - 1)], home_recv)
     arrived = home_in[...].reshape(2 * TILE, HEAD).astype(BF16)
     grad_ref[...] = dot(sorting[...], arrived, 0, 0).astype(BF16)
 
-    def sent_layer(layer):
-        @pl.when(layer % SECTIONS != z)
-        def _():
-            await_send(weight.at[layer, pl.ds(0, 2), :, 0], ring_send.at[layer, 0])
-            await_send(weight.at[layer, 0, :, 0], ring_send.at[layer, 1])
-            await_send(weight.at[layer, :, :, 0], ring_send.at[layer, 2])
-            await_send(packed_all.at[layer], packed_send.at[layer // SECTIONS, layer % SECTIONS])
-            await_send(pairs_all.at[layer], pair_send.at[layer // SECTIONS, layer % SECTIONS])
-
-    loop(0, LAYERS, sent_layer)
-
-    def sent_line(s):
-        await_send(gains.at[0], zg_right.at[s])
-        for v in range(2):
-            await_send(row_of(0, 0), zw_right.at[v, s])
-
-        @pl.when(s <= 6)
-        def _():
-            await_send(gains.at[0], zg_left.at[s])
-            for v in range(2):
-                await_send(row_of(0, 1), zw_left.at[v, s])
-
-    loop(0, 8, sent_line)
-
-    def sent_plane(k):
-        to = (d + k) % GROUPS
-        await_send(half_out.at[to], half_send.at[to])
-        await_send(home_out.at[to], home_send.at[to])
-
-    def sent_sections(k):
-        to = (z + k) % SECTIONS
-        await_send(rows_out.at[to], rows_send.at[to])
-        await_send(back_out.at[to], back_send.at[to])
-
-    loop(1, GROUPS, sent_plane)
-    loop(1, SECTIONS, sent_sections)
-
+    others = pl.ds(0, SECTIONS - 1)
+    for v in range(2):
+        await_send(weight.at[others, pl.ds(0, 2), :, 0], ring_send.at[v, 0])
+        await_send(weight.at[others, 0, :, 0], ring_send.at[v, 1])
+        await_send(weight.at[others, :, :, 0], ring_send.at[v, 2])
+        await_send(weight.at[pl.ds(0, 8), 0, :, 0], zw_right.at[v])
+        await_send(weight.at[pl.ds(0, 7), 0, :, 0], zw_left.at[v])
+        await_send(packed_all.at[others], packed_send.at[v])
+        await_send(pairs_all.at[others], pair_send.at[v])
+    await_send(gains.at[pl.ds(0, 8)], zg_right)
+    await_send(gains.at[pl.ds(0, 7)], zg_left)
+    await_send(rows_out.at[others], rows_send)
+    await_send(back_out.at[others], back_send)
+    await_send(half_out.at[pl.ds(0, GROUPS - 1)], half_send)
+    await_send(home_out.at[pl.ds(0, GROUPS - 1)], home_send)
     for v in range(2):
         await_send(twin_in.at[v], twin_send.at[v])
 
-        def await_chip(k):
-            at = (chip + k) % (GROUPS // 2)
-            await_recv(chip_in.at[v, at], chip_recv.at[v, at])
-            await_send(chip_terms.at[v, at], chip_send.at[v, at])
-
-        loop(1, GROUPS // 2, await_chip)
+        await_recv(chip_in.at[v, others], chip_recv.at[v])
+        await_send(chip_terms.at[v, others], chip_send.at[v])
         total = jnp.zeros((PART, 2 * HEAD), F32)
         for k in range(GROUPS // 2):
             total = total + chip_in[v, k].astype(F32)
@@ -624,13 +580,13 @@
             large, large, small, small, small, small, large, large,
             pltpu.VMEM((2 * ROWS, FEATURES), BF16),
             dma(()), dma((2, 2)),
-            dma((2, SECTIONS)), dma((2, 8)), dma((2, 8)),
-            dma((SECTIONS,)), dma((8,)), dma((8,)),
-            dma((LAYERS, 3)), dma((LAYERS, 5)),
-            dma((2, SECTIONS)), dma((2, SECTIONS)), dma((2, SECTIONS)), dma((2, SECTIONS)),
-            dma((GROUPS,)), dma((GROUPS,)), dma((SECTIONS,)), dma((SECTIONS,)),
-            dma((SECTIONS,)), dma((SECTIONS,)), dma((GROUPS,)), dma((GROUPS,)),
-            dma((2,)), dma((2,)), dma((2, chips)), dma((2, chips)),
+            dma((2, SECTIONS, SIDE)), dma((2,)), dma((2,)),
+            dma((SECTIONS,)), dma(()), dma(()),
+            dma((2, 3)), dma((LAYERS, 5)),
+            dma((2,)), dma((2,)), dma((2,)), dma((2,)),
+            dma(()), dma(()), dma(()), dma(()),
+            dma(()), dma(()), dma(()), dma(()),
+            dma((2,)), dma((2,)), dma((2,)), dma((2,)),
         ],
         compiler_params=pltpu.CompilerParams(
             collective_id=0, has_side_effects=True, vmem_limit_bytes=56 * 2**20),

time: 196 us -> 182 us (0.929)
  Pallas kernels: 192 us -> 178 us
    pallas_call x1, Pallas kernels: 192 us -> 178 us  [run_whole(): pl.pallas_call(whole_kernel, out_shape=(jax.ShapeDtypeStruct((TILE, HEAD)...]
where the time goes in v4:
time: 182 us; the launch traced here: 181 us
  Pallas kernels  178 us (98%)
  local copies, waits for them, and re-layouts  2.9 us (2%)
    pallas_call x1, Pallas kernels, run_whole(): pl.pallas_call(whole_kernel, out_shape=(jax.ShapeDtypeStruct((TILE, HEAD)...  178 us

profile of v4, /device:TPU:1, one launch (start us, length us, event | category | flops | bytes accessed | tf_op | source)
XLA Modules:
  0.0 181.3 jit_solution(11303936590708113951)
XLA Ops:
  0.6 177.8 %shard_map.94 = (bf16[128,128]{1,0:T(8,128)(2,1)}, f32[2,64,128]{2,1,0:T(8,128)}, f32[2,64,128]{2,1,0:T(8,128)}) custom-call(bf16[128,128]{1,0:T(8,128)(2,1)} %hidden_ref.1, s32[4,16]{1,0:T(4,128)} %bitcast.6, s32[2,16]{1,0:T(2,128)} %bitcast.7, f32[2,2048]{1,0:T(2,128)} %gain_ref.1, bf16[2,4,4,2,64,128]{5,4,3,2,1,0:T(8,128)(2,1)} %bitcast.4, ...), custom_call_target="tpu_custom_call" | custom-call | tf_op jit(solution)/shard_map/pallas_call | solution.py:550
  178.4 0.0 copy-start.1
  178.4 1.4 copy.13
  179.9 0.0 copy-done.1
  179.9 0.0 copy-start
  179.9 0.6 copy.14
  180.5 0.2 copy-done
  180.7 0.6 copy.15
Async XLA Ops:
  178.4 1.4 copy-start.1
  179.9 0.9 copy-start

commit v5 on v4

--- a/solution.py
+++ b/solution.py
@@ -168,7 +168,7 @@
         to = (d + k) % GROUPS
         remote(half_out.at[to], half_in.at[d], half_send, half_recv, z, to).start()
 
-    for copy in owned:
+    for copy in owned[:2]:
         copy.wait()
 
     def row_of(layer, e):
@@ -177,9 +177,10 @@
     def line_step(v, s):
         on_left = (z + SECTIONS - s) % SECTIONS
         on_right = (z + s) % SECTIONS
-        for q in range(SIDE):
-            left = weight.at[v * SECTIONS + on_left, q, py, core]
-            right = weight.at[v * SECTIONS + on_right, px, q, core]
+        for q in range(2):
+            two = pl.ds(2 * q, 2)
+            left = weight.at[v * SECTIONS + on_left, two, py, core]
+            right = weight.at[v * SECTIONS + on_right, px, two, core]
             left_sem = zw_recv.at[v, on_left, q]
             right_sem = zw_recv.at[v, on_right, q]
 
@@ -224,6 +225,8 @@
     line_step(0, 0)
     gain_step(0)
     loop(1, GROUPS, send_half)
+    for copy in owned[2:]:
+        copy.wait()
 
     def send_rows(k):
         to = (z + k) % SECTIONS
@@ -372,7 +375,7 @@
             def _():
                 stage(v * SECTIONS + (z + s) % SECTIONS, 1)
 
-        @pl.when(t == 3)
+        @pl.when(t == 9)
         def _():
             place_halves()
 
@@ -476,16 +479,14 @@
         def _():
             send_pairs(1, 2 * (j - SECTIONS) + 2)
 
-        @pl.when(j == 27)
-        def _():
-            terms_of(1)
-
-        @pl.when(j == 30)
-        def _():
-            send_chips(1)
+        layer = LAYERS - 1 - j
+
+        @pl.when((j >= SECTIONS) & (layer != z))
+        def _():
+            remote(pairs_all.at[layer], pairs_in.at[0, z],
+                   pair_send.at[0], pair_recv.at[0], layer, d).start()
 
     loop(0, LAYERS, backward_step)
-    loop(1, SECTIONS, lambda j: send_pairs(0, j))
 
     back_out[...] = current[...].astype(BF16).astype(F32).reshape(SECTIONS, ROWS, HEAD)
     back_in[z] = back_out[z]
@@ -495,6 +496,7 @@
         remote(back_out.at[to], back_in.at[z], back_send, back_recv, to, d).start()
 
     loop(1, SECTIONS, send_back)
+    terms_of(1)
     terms_of(0)
 
     await_recv(back_in.at[pl.ds(0, SECTIONS - 1)], back_recv)
@@ -507,6 +509,7 @@
         remote(home_out.at[to], home_in.at[d], home_send, home_recv, z, to).start()
 
     loop(1, GROUPS, send_home)
+    send_chips(1)
     send_chips(0)
 
     await_recv(home_in.at[pl.ds(0, GROUPS - 1)], home_recv)
@@ -580,7 +583,7 @@
             large, large, small, small, small, small, large, large,
             pltpu.VMEM((2 * ROWS, FEATURES), BF16),
             dma(()), dma((2, 2)),
-            dma((2, SECTIONS, SIDE)), dma((2,)), dma((2,)),
+            dma((2, SECTIONS, 2)), dma((2,)), dma((2,)),
             dma((SECTIONS,)), dma(()), dma(()),
             dma((2, 3)), dma((LAYERS, 5)),
             dma((2,)), dma((2,)), dma((2,)), dma((2,)),

time: 182 us -> 176 us (0.967)
  Pallas kernels: 178 us -> 172 us
    pallas_call x1, Pallas kernels: 178 us -> 172 us  [run_whole(): pl.pallas_call(whole_kernel, out_shape=(jax.ShapeDtypeStruct((TILE, HEAD)...]
where the time goes in v5:
time: 176 us; the launch traced here: 175 us
  Pallas kernels  172 us (98%)
  local copies, waits for them, and re-layouts  2.9 us (2%)
    pallas_call x1, Pallas kernels, run_whole(): pl.pallas_call(whole_kernel, out_shape=(jax.ShapeDtypeStruct((TILE, HEAD)...  172 us

profile of v5, /device:TPU:1, one launch (start us, length us, event | category | flops | bytes accessed | tf_op | source)
XLA Modules:
  0.0 175.3 jit_solution(12759411841588135743)
XLA Ops:
  0.6 171.7 %shard_map.94 = (bf16[128,128]{1,0:T(8,128)(2,1)}, f32[2,64,128]{2,1,0:T(8,128)}, f32[2,64,128]{2,1,0:T(8,128)}) custom-call(bf16[128,128]{1,0:T(8,128)(2,1)} %hidden_ref.1, s32[4,16]{1,0:T(4,128)} %bitcast.6, s32[2,16]{1,0:T(2,128)} %bitcast.7, f32[2,2048]{1,0:T(2,128)} %gain_ref.1, bf16[2,4,4,2,64,128]{5,4,3,2,1,0:T(8,128)(2,1)} %bitcast.4, ...), custom_call_target="tpu_custom_call" | custom-call | tf_op jit(solution)/shard_map/pallas_call | solution.py:553
  172.3 0.0 copy-start.1
  172.4 1.4 copy.13
  173.8 0.0 copy-done.1
  173.8 0.0 copy-start
  173.8 0.6 copy.14
  174.4 0.2 copy-done
  174.6 0.6 copy.15
Async XLA Ops:
  172.3 1.4 copy-start.1
  173.8 0.9 copy-start

commit v6 on v5

--- a/solution.py
+++ b/solution.py
@@ -498,6 +498,7 @@
     loop(1, SECTIONS, send_back)
     terms_of(1)
     terms_of(0)
+    send_chips(1)
 
     await_recv(back_in.at[pl.ds(0, SECTIONS - 1)], back_recv)
     mine = back_in[...].reshape(TILE, HEAD).astype(BF16)
@@ -509,7 +510,6 @@
         remote(home_out.at[to], home_in.at[d], home_send, home_recv, z, to).start()
 
     loop(1, GROUPS, send_home)
-    send_chips(1)
     send_chips(0)
 
     await_recv(home_in.at[pl.ds(0, GROUPS - 1)], home_recv)

time: 176 us -> 176 us (level)
  no operation moved by 1% of the time
where the time goes in v6:
time: 176 us; the launch traced here: 174 us
  Pallas kernels  171 us (97%)
  local copies, waits for them, and re-layouts  2.9 us (2%)
    pallas_call x1, Pallas kernels, run_whole(): pl.pallas_call(whole_kernel, out_shape=(jax.ShapeDtypeStruct((TILE, HEAD)...  171 us

profile of v6, /device:TPU:1, one launch (start us, length us, event | category | flops | bytes accessed | tf_op | source)
XLA Modules:
  0.0 174.4 jit_solution(1609482633083407773)
XLA Ops:
  0.6 170.9 %shard_map.94 = (bf16[128,128]{1,0:T(8,128)(2,1)}, f32[2,64,128]{2,1,0:T(8,128)}, f32[2,64,128]{2,1,0:T(8,128)}) custom-call(bf16[128,128]{1,0:T(8,128)(2,1)} %hidden_ref.1, s32[4,16]{1,0:T(4,128)} %bitcast.6, s32[2,16]{1,0:T(2,128)} %bitcast.7, f32[2,2048]{1,0:T(2,128)} %gain_ref.1, bf16[2,4,4,2,64,128]{5,4,3,2,1,0:T(8,128)(2,1)} %bitcast.4, ...), custom_call_target="tpu_custom_call" | custom-call | tf_op jit(solution)/shard_map/pallas_call | solution.py:553
  171.5 0.0 copy-start.1
  171.5 1.4 copy.13
  172.9 0.0 copy-done.1
  173.0 0.0 copy-start
  173.0 0.6 copy.14
  173.6 0.2 copy-done
  173.8 0.6 copy.15
Async XLA Ops:
  171.5 1.4 copy-start.1
  173.0 0.9 copy-start
